TPU v7x, 256 devices: a whole 4x4x8 slice. The times are simulated.
256 devices in a mesh: dom: 64 (over z_hi, x, y), band: 4 (over z_lo, core).
Axes of the slice: x: 4, y: 4, z: 8 (z_hi: 4, z_lo: 2; z = z_hi * 2 + z_lo), core: 2. Of those that a mesh axis runs over, the one named last changes fastest.
Arguments:
- wavefunctions: float32 [16384, 512], P('dom', 'band'), may hold values from -6 to 6
- node_mass: float32 [16384], P('dom'), may hold values from 1 to 2
- cell_potential: float32 [16384], P('dom'), may hold values from 0 to 2
- cell_nodes: int32 [8, 16384], P(None, 'dom'), may hold values from 0 to 319, as said below
- plane_nodes: int32 [4096], P('dom'), may hold values from 0 to 255, as said below
- state_order: int32 [512], replicated, may hold values from 0 to 511, each once
Outputs:
- filtered: float32 [16384, 512], P('dom', 'band')
- margin: float32 [512, 512], P('dom', 'band')
Inputs may be any that keep to these rules, and one draw needn't show every extreme that they name: `cell_nodes`: in each partition, cell c has its corners in node layers c // 64 and c // 64 + 1. An entry below 256 is a row of the partition's own block; an entry 256 + q is the q-th node named by the next partition's plane_nodes. Only cells c >= 192 of a partition have such entries. Every own row is a corner of some cell. `plane_nodes`: each partition's 64 entries are distinct rows of its own block, all in its first node layer.
All inputs are finite; a program needn't handle non-finite values.
Results may differ from a plain program's by a relative error of at most 0.0001.
Values sent between devices are 32-bit elements; how exact they have to be, the bound alone decides.
No kernel may reach another device: no remote copies, remote signals or barrier semaphores. Data moves between devices by JAX's collectives and lax.ppermute only.
A program may use at most 64 MiB of HBM per device.

v0:
```python
import jax
import jax.numpy as jnp
import numpy as np
from jax import lax
from jax.sharding import PartitionSpec as P

DEGREE = 8


lower_cut = 1.5
upper_edge = 5.0
anchor_value = 0.4


def passed_along(block, axis, distance):
    devices = range(lax.axis_size(axis))
    route = [(i - distance, i) for i in devices if i - distance in devices]
    return lax.ppermute(block, axis, route)


def cell_tables():
    stiff_line = np.array([[1.0, -1.0], [-1.0, 1.0]])
    mass_line = np.array([[1.0 / 3.0, 1.0 / 6.0], [1.0 / 6.0, 1.0 / 3.0]])
    stiffness = np.kron(np.kron(stiff_line, mass_line), mass_line)
    stiffness = stiffness + np.kron(np.kron(mass_line, stiff_line), mass_line)
    stiffness = stiffness + np.kron(np.kron(mass_line, mass_line), stiff_line)
    cell_mass = np.kron(np.kron(mass_line, mass_line), mass_line)
    return np.concatenate([0.5 * stiffness, cell_mass], 0).astype(np.float32)


def contributions(source, links, potential, cell_table):
    state_width = source.shape[1]
    cell_count = links.shape[1]
    gathered = source[links.reshape(-1)].reshape(8, cell_count * state_width)
    mixed = jnp.dot(
        cell_table, gathered, precision=lax.Precision.HIGHEST, preferred_element_type=jnp.float32
    ).reshape(16, cell_count, state_width)
    return mixed[:8] + potential[None, :, None] * mixed[8:]


def accumulate(result, links, contrib):
    return result.at[links.reshape(-1)].add(contrib.reshape(-1, contrib.shape[2]))


def shards(wavefunctions, node_mass, cell_potential, cell_nodes, plane_nodes, state_order):
    cell_table = jnp.asarray(cell_tables(), jnp.float32)
    node_scale = lax.rsqrt(node_mass)[:, None]
    node_count = wavefunctions.shape[0]
    plane_count = plane_nodes.shape[0]

    def hamiltonian(field_values):
        weighted = node_scale * field_values
        boundary = weighted[plane_nodes]
        ghost_plane = passed_along(boundary, "dom", -1)
        result = jnp.zeros((node_count + plane_count, field_values.shape[1]), jnp.float32)
        extended = jnp.concatenate([weighted, ghost_plane], 0)
        result = accumulate(
            result, cell_nodes, contributions(extended, cell_nodes, cell_potential, cell_table)
        )
        returned = passed_along(result[node_count:], "dom", 1)
        owned_result = result[:node_count].at[plane_nodes].add(returned)
        return node_scale * owned_result

    half_span = (upper_edge - lower_cut) / 2.0
    center = (upper_edge + lower_cut) / 2.0
    sigma_first = half_span / (anchor_value - center)
    gamma_value = 2.0 / sigma_first
    previous = wavefunctions
    current = sigma_first / half_span * (hamiltonian(previous) - center * previous)
    sigma_last = sigma_first
    for degree_index in range(2, DEGREE + 1):
        sigma_next = 1.0 / (gamma_value - sigma_last)
        following = 2.0 * sigma_next / half_span * (hamiltonian(current) - center * current)
        following = following - sigma_last * sigma_next * previous
        previous = current
        current = following
        sigma_last = sigma_next
    all_states = lax.all_gather(current, "band", axis=1, tiled=True)
    permuted = jnp.take(all_states, state_order, axis=1)
    state_width = current.shape[1]
    own_columns = lax.dynamic_slice_in_dim(
        permuted, lax.axis_index("band") * state_width, state_width, 1
    )
    row_count = state_order.shape[0] // lax.axis_size("dom")
    total_nodes = node_count * lax.axis_size("dom")
    term_part = jnp.dot(
        permuted.T, own_columns, precision=lax.Precision.HIGHEST, preferred_element_type=jnp.float32
    )
    summed = lax.psum(term_part, "dom")
    own_block = lax.dynamic_slice_in_dim(summed, lax.axis_index("dom") * row_count, row_count, 0)
    return (current, own_block / total_nodes)


def solution(mesh):
    in_specs = (P("dom", "band"), P("dom"), P("dom"), P(None, "dom"), P("dom"), P())
    out_specs = (P("dom", "band"), P("dom", "band"))
    return jax.shard_map(shards, mesh=mesh, in_specs=in_specs, out_specs=out_specs, check_vma=False)
```

profile of v0, /device:TPU:32, one launch (start us, length us, event | category | flops | bytes accessed | tf_op | source)
XLA Modules:
  0.0 1030.1 jit_solution(9238209826197385065)
XLA Ops:
  16.0 5.5 gather_fusion.1
  24.5 12.5 %scatter_custom_fusion = f32[320,128]{1,0:T(8,128)S(1)} fusion(s32[2048]{0:T(1024)S(1)} %bitcast.34, f32[2048,128]{1,0:T(8,128)S(1)} %slice.145, f32[2048,128]{1,0:T(8,128)S(1)} %slice.147, f32[2048]{0:T(1024)S(1)} %bitcast.25, f32[]{:T(128)} %constant.31.clone.1), kind=kCustom, calls=%fused_computation.54 | custom fusion | flops 786432 | bytes 2269188 | tf_op jit(solution)/shard_map/scatter-add | solution.py:42
  49.9 5.5 gather_fusion.3
  57.9 12.5 %scatter_custom_fusion.2 = f32[320,128]{1,0:T(8,128)S(1)} fusion(s32[2048]{0:T(1024)S(1)} %bitcast.35, f32[2048,128]{1,0:T(8,128)S(1)} %slice.151, f32[2048,128]{1,0:T(8,128)S(1)} %slice.153, f32[2048]{0:T(1024)S(1)} %bitcast.26, f32[]{:T(128)} %constant.31.clone.1), kind=kCustom, calls=%fused_computation.51 | custom fusion | flops 786432 | bytes 2269188 | tf_op jit(solution)/shard_map/scatter-add | solution.py:42
  84.4 5.5 gather_fusion.5
  92.4 12.7 %scatter_custom_fusion.4 = f32[320,128]{1,0:T(8,128)S(1)} fusion(s32[2048]{0:T(1024)} %bitcast.36, f32[2048,128]{1,0:T(8,128)S(1)} %slice.157, f32[2048,128]{1,0:T(8,128)S(1)} %slice.159, f32[2048]{0:T(1024)S(1)} %bitcast.27, f32[]{:T(128)} %constant.31.clone.1), kind=kCustom, calls=%fused_computation.48 | custom fusion | flops 786432 | bytes 2269696 | tf_op jit(solution)/shard_map/scatter-add | solution.py:42
  105.1 6.0 collective-permute-start.5
  121.3 5.5 gather_fusion.7
  129.8 12.8 %scatter_custom_fusion.6 = f32[320,128]{1,0:T(8,128)S(1)} fusion(s32[2048]{0:T(1024)} %bitcast.37, f32[2048,128]{1,0:T(8,128)S(1)} %slice.163, f32[2048,128]{1,0:T(8,128)S(1)} %slice.165, f32[2048]{0:T(1024)S(1)} %bitcast.28, f32[]{:T(128)} %constant.31.clone.1), kind=kCustom, calls=%fused_computation.45 | custom fusion | flops 786432 | bytes 2269696 | tf_op jit(solution)/shard_map/scatter-add | solution.py:42
  142.6 6.0 collective-permute-start.7
  158.2 5.5 gather_fusion.9
  166.6 12.8 %scatter_custom_fusion.8 = f32[320,128]{1,0:T(8,128)S(1)} fusion(s32[2048]{0:T(1024)} %bitcast.38, f32[2048,128]{1,0:T(8,128)S(1)} %slice.169, f32[2048,128]{1,0:T(8,128)S(1)} %slice.171, f32[2048]{0:T(1024)S(1)} %bitcast.29, f32[]{:T(128)} %constant.31.clone.1), kind=kCustom, calls=%fused_computation.42 | custom fusion | flops 786432 | bytes 2269696 | tf_op jit(solution)/shard_map/scatter-add | solution.py:42
  179.4 6.0 collective-permute-start.9
  195.0 5.5 gather_fusion.11
  203.0 12.7 %scatter_custom_fusion.10 = f32[320,128]{1,0:T(8,128)S(1)} fusion(s32[2048]{0:T(1024)} %bitcast.39, f32[2048,128]{1,0:T(8,128)S(1)} %slice.175, f32[2048,128]{1,0:T(8,128)S(1)} %slice.177, f32[2048]{0:T(1024)S(1)} %bitcast.30, f32[]{:T(128)} %constant.31.clone.1), kind=kCustom, calls=%fused_computation.39 | custom fusion | flops 786432 | bytes 2269696 | tf_op jit(solution)/shard_map/scatter-add | solution.py:42
  215.6 6.0 collective-permute-start.11
  231.2 5.5 gather_fusion.13
  239.7 12.7 %scatter_custom_fusion.12 = f32[320,128]{1,0:T(8,128)S(1)} fusion(s32[2048]{0:T(1024)} %bitcast.40, f32[2048,128]{1,0:T(8,128)S(1)} %slice.181, f32[2048,128]{1,0:T(8,128)S(1)} %slice.183, f32[2048]{0:T(1024)S(1)} %bitcast.31, f32[]{:T(128)} %constant.31.clone.1), kind=kCustom, calls=%fused_computation.36 | custom fusion | flops 786432 | bytes 2269696 | tf_op jit(solution)/shard_map/scatter-add | solution.py:42
  252.3 6.0 collective-permute-start.13
  267.9 5.5 gather_fusion.15
  276.4 12.7 %scatter_custom_fusion.14 = f32[320,128]{1,0:T(8,128)S(1)} fusion(s32[2048]{0:T(1024)} %bitcast.41, f32[2048,128]{1,0:T(8,128)S(1)} %slice.187, f32[2048,128]{1,0:T(8,128)S(1)} %slice.189, f32[2048]{0:T(1024)S(1)} %bitcast.32, f32[]{:T(128)} %constant.31.clone.1), kind=kCustom, calls=%fused_computation.33 | custom fusion | flops 786432 | bytes 2269696 | tf_op jit(solution)/shard_map/scatter-add | solution.py:42
  289.0 6.0 collective-permute-start.15
  297.8 6.5 all_gather.3
  307.6 714.2 %all-reduce.2.cloned.1.call-done = f32[512,128]{1,0:T(8,128)} async-done(((f32[512,128]{1,0:T(8,128)}), f32[512,128]{1,0:T(8,128)}) %all-reduce.2.cloned.1.call-update) | async-done | bytes 262160 | tf_op jit(solution)/shard_map/psum | solution.py:89
  (183 shorter events, 112.8 us)
Async XLA Ops:
  7.2 1014.6 %all-reduce.2.cloned.1.call-start = ((), (), s32[]{:S(2)}) async-start(), calls=%async_computation | async-start | bytes 524288 | tf_op jit(solution)/shard_map/psum | solution.py:89
  8.6 68.0 %copy-start.17 = (s32[64]{0:T(128)}, s32[64]{0:T(128)S(1)}, u32[]{:S(2)}) copy-start(s32[64]{0:T(128)S(1)} %compare_select_fusion.2) | copy-start | bytes 772
  8.6 69.1 %copy-start.20 = (s32[1024]{0:T(1024)}, s32[1024]{0:T(1024)S(1)}, u32[]{:S(2)}) copy-start(s32[1024]{0:T(1024)S(1)} %pad_clamp_fusion.1) | copy-start | bytes 12292
  10.2 5.8 collective-permute-start
  12.2 45.6 %copy-start.19 = (s32[2048,1]{0,1:T(1,128)}, s32[2048,1]{0,1:T(1,128)S(1)}, u32[]{:S(2)}) copy-start(s32[2048,1]{0,1:T(1,128)S(1)} %compare_select_fusion) | copy-start | bytes 24580
  12.3 72.2 %copy-start.5 = (s32[2048]{0:T(1024)}, s32[2048]{0:T(1024)S(1)}, u32[]{:S(2)}) copy-start(s32[2048]{0:T(1024)S(1)} %broadcast_clamp_fusion) | copy-start | bytes 24580
  37.0 5.1 collective-permute-start.1
  43.8 6.1 collective-permute-start.2
  70.4 6.1 collective-permute-start.3
  78.3 6.1 collective-permute-start.4
  92.4 28.9 %copy-start.6 = (s32[2048]{0:T(1024)S(1)}, s32[2048]{0:T(1024)}, u32[]{:S(2)}) copy-start(s32[2048]{0:T(1024)} %copy-done.5) | copy-start | bytes 24580
  105.1 7.6 collective-permute-start.5
  115.2 6.1 collective-permute-start.6
  129.8 28.4 %copy-start.7 = (s32[2048]{0:T(1024)S(1)}, s32[2048]{0:T(1024)}, u32[]{:S(2)}) copy-start(s32[2048]{0:T(1024)} %copy-done.5) | copy-start | bytes 24580
  142.6 7.6 collective-permute-start.7
  152.0 6.1 collective-permute-start.8
  179.4 7.6 collective-permute-start.9
  188.9 6.1 collective-permute-start.10
  215.6 7.6 collective-permute-start.11
  225.1 6.1 collective-permute-start.12
  252.3 7.6 collective-permute-start.13
  261.8 6.1 collective-permute-start.14
  289.0 7.6 collective-permute-start.15
  304.5 718.6 %copy-start.1 = (f32[256]{0:T(256)S(1)}, f32[256]{0:T(256)}, u32[]{:S(2)}) copy-start(f32[256]{0:T(256)} %param.9) | copy-start | bytes 3076
  (18 other events, 246.4 us)
Sparse Core Ops, SparseCore 0:
  307.7 714.0 all-reduce.1
where the time goes:
time: 1040 us; the launch traced here: 1030 us
  waiting for transfers between devices  762 us (73%)
  other arithmetic  116 us (11%)
  local copies, waits for them, and re-layouts  59.5 us (6%)
  starting transfers between devices  55.4 us (5%)
  matrix products  15.5 us (1%)
  between operations  15.5 us (1%)
    psum x1, waiting for transfers between devices, shards(): summed = lax.psum(term_part, 'dom')  714 us
    scatter-add x8, other arithmetic, accumulate(): result.at[links.reshape(-1)].add(contrib.reshape(-1, contrib.shape[2]))  101 us
    ppermute x16, starting transfers between devices, passed_along(): return lax.ppermute(block, axis, route)  55.4 us
    ppermute x16, waiting for transfers between devices, passed_along(): return lax.ppermute(block, axis, route)  47.9 us
    gather x8, local copies, waits for them, and re-layouts, contributions(): gathered = source[links.reshape(-1)].reshape(8, cell_count * state_width)  43.7 us
  transfers between devices with their start and end apart: 17, of which 17 were waited for; matrix products, arithmetic and copies ran while one was open for 0% of the time, Pallas kernels for 0%

commit v1 on v0

v1 whole, which is shorter than its diff:
```python
import jax
import jax.numpy as jnp
import numpy as np
from jax import lax
from jax.experimental import pallas as pl
from jax.experimental.pallas import tpu as pltpu
from jax.sharding import PartitionSpec as P

DEGREE = 8
REACH = 2
WINDOW = 2 * REACH + 1

lower_cut = 1.5
upper_edge = 5.0
anchor_value = 0.4

half_span = (upper_edge - lower_cut) / 2.0
center = (upper_edge + lower_cut) / 2.0

VMEM = pl.BlockSpec(memory_space=pltpu.VMEM)
SMEM = pl.BlockSpec(memory_space=pltpu.SMEM)
f32 = jnp.float32
bf16 = jnp.bfloat16


def dot(a, b):
    return lax.dot_general(a, b, (((1,), (0,)), ((), ())), preferred_element_type=f32)


def dot_t(a, b):
    return lax.dot_general(a, b, (((1,), (1,)), ((), ())), preferred_element_type=f32)


def split(x):
    high = x.astype(bf16)
    return high, (x - high.astype(f32)).astype(bf16)


def corner_mix(corners, potential):
    total = corners[0]
    for item in corners[1:]:
        total = total + item
    mass = list(corners)
    for bit in (1, 2, 4):
        mixed = [None] * 8
        for a in range(8):
            if not a & bit:
                pair = mass[a] + mass[a | bit]
                mixed[a] = mass[a] + pair
                mixed[a | bit] = mass[a | bit] + pair
        mass = mixed
    result = []
    for a in range(8):
        near = corners[a ^ 1] + corners[a ^ 2] + corners[a ^ 4]
        stiff = 5 * corners[a] + near - total
        result.append(stiff.astype(f32) * (1.0 / 24.0) + mass[a].astype(f32) * (potential * (1.0 / 216.0)))
    return result


def build_kernel(place, own, r1, l1, r2, l2, high_ref, low_ref, nn_ref):
    position, last = place[0], place[2]
    blocks = {REACH - 2: l2, REACH - 1: l1, REACH: own, REACH + 1: r1, REACH + 2: r2}
    nodes = own.shape[1]
    row_id = lax.broadcasted_iota(jnp.int32, (nodes, nodes), 0).astype(f32)
    col_id = lax.broadcasted_iota(jnp.int32, (nodes, nodes), 1).astype(f32)
    diagonal = row_id == col_id
    ghost_id = row_id[:128, :128] + float(nodes)

    def exists(q):
        where = position + (q - REACH)
        return jnp.logical_and(where >= 0, where <= last)

    scale_row, scale_col = [], []
    for q in range(WINDOW):
        mass = jnp.where(exists(q), blocks[q][9:10, :], 1.0)
        row = lax.rsqrt(mass)
        scale_row.append(row)
        scale_col.append(jnp.sum(jnp.where(diagonal, row, 0.0), axis=1, keepdims=True))
    for q in range(WINDOW):
        block = blocks[q]
        potential = block[8:9, :]
        corners = [jnp.where(row_id == block[a : a + 1, :], 1.0, 0.0).astype(bf16) for a in range(8)]
        mixed = corner_mix(corners, potential)
        own_own = jnp.zeros((nodes, nodes), f32)
        for a in range(8):
            high, low = split(mixed[a])
            own_own = own_own + dot_t(corners[a], high) + dot_t(corners[a], low)
        if q > 0:
            own_own = own_own + nn_ref[...]
        mid = own_own * (scale_col[q] * (1.0 / half_span)) * scale_row[q]
        mid = mid - jnp.where(diagonal, center / half_span, 0.0)
        high, low = split(mid)
        high_ref[q, :, nodes : 2 * nodes] = high
        low_ref[q, :, nodes : 2 * nodes] = low
        if q + 1 < WINDOW:
            joined = jnp.where(jnp.logical_and(exists(q), exists(q + 1)), 1.0, 0.0)
            tail = nodes - 128
            ghosts = [
                jnp.where(ghost_id == block[a : a + 1, tail:], 1.0, 0.0).astype(bf16) for a in range(8)
            ]
            ghost_mixed = corner_mix(ghosts, potential[:, tail:])
            og = jnp.zeros((nodes, 128), f32)
            gg = jnp.zeros((128, 128), f32)
            for a in range(8):
                high, low = split(ghost_mixed[a])
                tail_corner = corners[a][:, tail:]
                og = og + dot_t(tail_corner, high) + dot_t(tail_corner, low)
                gg = gg + dot_t(ghosts[a], high) + dot_t(ghosts[a], low)
            og = og * joined
            gg = gg * joined
            place_next = jnp.where(row_id[:, :128] == blocks[q + 1][10:11, :128], 1.0, 0.0).astype(bf16)
            og_high, og_low = split(og)
            up = dot_t(og_high, place_next) + dot_t(og_low, place_next)
            down = dot_t(place_next, og_high) + dot_t(place_next, og_low)
            gg_high, gg_low = split(gg)
            half_high = dot(place_next, gg_high).astype(bf16)
            half_low = dot(place_next, gg_low).astype(bf16)
            nn_ref[...] = dot_t(half_high, place_next) + dot_t(half_low, place_next)
            up = up * (scale_col[q] * (1.0 / half_span)) * scale_row[q + 1]
            down = down * (scale_col[q + 1] * (1.0 / half_span)) * scale_row[q]
            high, low = split(up)
            high_ref[q, :, 2 * nodes :] = high
            low_ref[q, :, 2 * nodes :] = low
            high, low = split(down)
            high_ref[q + 1, :, :nodes] = high
            low_ref[q + 1, :, :nodes] = low


def filter_kernel(place, own, near_a, near_b, far_a, far_b, high_ref, low_ref, out, even, odd, field_a, field_b):
    position = place[0]
    nodes, width = own.shape
    is_even = lax.rem(position, 2) == 0
    is_low = lax.rem(position, 4) < 2
    first = [
        jnp.where(is_low, far_b[...], far_a[...]),
        jnp.where(is_even, near_b[...], near_a[...]),
        own[...],
        jnp.where(is_even, near_a[...], near_b[...]),
        jnp.where(is_low, far_a[...], far_b[...]),
    ]

    def put(target, q, value):
        high, low = split(value)
        target[nodes * q : nodes * (q + 1), :width] = high
        target[nodes * q : nodes * (q + 1), width:] = low

    for q in range(WINDOW):
        field_a[q] = first[q]
        put(even, q, first[q])
    sigma_first = half_span / (anchor_value - center)
    gamma_value = 2.0 / sigma_first
    sigma_last = sigma_first
    layers = 4
    for k in range(1, DEGREE + 1):
        source, target = (even, odd) if k % 2 else (odd, even)
        older, newer = (field_a, field_b) if k % 2 else (field_b, field_a)
        if k == 1:
            gain, keep = sigma_first, None
        else:
            sigma_next = 1.0 / (gamma_value - sigma_last)
            gain, keep = 2.0 * sigma_next, sigma_last * sigma_next
            sigma_last = sigma_next
        reach = -(-(DEGREE - k) // layers)
        for q in range(REACH - reach, REACH + reach + 1):
            start, stop = max(q - 1, 0), min(q + 2, WINDOW)
            left, right = nodes * (start - q + 1), nodes * (stop - q + 1)
            rows = slice(nodes * start, nodes * stop)
            main = dot(high_ref[q, :, left:right], source[rows, :])
            rest = dot(low_ref[q, :, left:right], source[rows, :width])
            value = gain * (main[:, :width] + main[:, width:] + rest)
            if keep is not None:
                value = value - keep * newer[q]
            if k == DEGREE:
                out[...] = value
            else:
                newer[q] = value
                put(target, q, value)


def margin_kernel(place, states, order, out):
    band = place[1]
    count = order.shape[1]
    width = out.shape[1]
    state_id = lax.broadcasted_iota(jnp.int32, (count, count), 0)
    pick = jnp.where(state_id == order[...], 1.0, 0.0).astype(bf16)
    high, low = split(states[...])
    high = dot(high, pick)
    low = dot(low, pick).astype(bf16)
    high = high.astype(bf16)
    own_order = order[:, pl.ds(pl.multiple_of(band * width, width), width)]
    own_pick = jnp.where(state_id[:, :width] == own_order, 1.0, 0.0).astype(bf16)
    own_high, own_low = split(states[...])
    own_high = dot(own_high, own_pick).astype(bf16)
    own_low = dot(own_low, own_pick).astype(bf16)

    def cross(a, b):
        return lax.dot_general(a, b, (((0,), (0,)), ((), ())), preferred_element_type=f32)

    out[...] = cross(high, own_high) + cross(high, own_low) + cross(low, own_high)


def swapped(block, axis, pairs):
    count = lax.axis_size(axis)
    route = [
        step for a, b in pairs if a < count and b < count for step in ((a, b), (b, a))
    ]
    return lax.ppermute(block, axis, route)


def shards(wavefunctions, node_mass, cell_potential, cell_nodes, plane_nodes, state_order):
    nodes, width = wavefunctions.shape
    doms = lax.axis_size("dom")
    place = jnp.stack([lax.axis_index("dom"), lax.axis_index("band"), doms - 1]).astype(jnp.int32)
    position = lax.axis_index("dom")
    plane_row = jnp.pad(plane_nodes.astype(f32), (0, nodes - plane_nodes.shape[0]), constant_values=-1.0)
    small = jnp.concatenate(
        [
            cell_nodes.astype(f32),
            cell_potential[None, :],
            node_mass[None, :],
            plane_row[None, :],
            jnp.zeros((5, nodes), f32),
        ],
        0,
    )
    near_pairs = [
        [(2 * i, 2 * i + 1) for i in range(doms)],
        [(2 * i + 1, 2 * i + 2) for i in range(doms)],
    ]
    far_pairs = [
        [(4 * i + j, 4 * i + j + 2) for i in range(doms) for j in range(2)],
        [(4 * i + j + 2, 4 * i + j + 4) for i in range(doms) for j in range(2)],
    ]
    routes = near_pairs + far_pairs
    small_got = [swapped(small, "dom", route) for route in routes]
    field_got = [swapped(wavefunctions, "dom", route) for route in routes]
    is_even = position % 2 == 0
    is_low = position % 4 < 2
    small_r1 = jnp.where(is_even, small_got[0], small_got[1])
    small_l1 = jnp.where(is_even, small_got[1], small_got[0])
    small_r2 = jnp.where(is_low, small_got[2], small_got[3])
    small_l2 = jnp.where(is_low, small_got[3], small_got[2])

    high, low = pl.pallas_call(
        build_kernel,
        out_shape=[jax.ShapeDtypeStruct((WINDOW, nodes, 3 * nodes), bf16)] * 2,
        in_specs=[SMEM] + [VMEM] * 5,
        out_specs=[VMEM] * 2,
        scratch_shapes=[pltpu.VMEM((nodes, nodes), f32)],
        compiler_params=pltpu.CompilerParams(vmem_limit_bytes=40 * 2**20),
        cost_estimate=pl.CostEstimate(flops=8_000_000_000, bytes_accessed=4_000_000, transcendentals=0),
        name="build",
    )(place, small, small_r1, small_l1, small_r2, small_l2)

    filtered = pl.pallas_call(
        filter_kernel,
        out_shape=jax.ShapeDtypeStruct((nodes, width), f32),
        in_specs=[SMEM] + [VMEM] * 7,
        out_specs=VMEM,
        scratch_shapes=[
            pltpu.VMEM((WINDOW * nodes, 2 * width), bf16),
            pltpu.VMEM((WINDOW * nodes, 2 * width), bf16),
            pltpu.VMEM((WINDOW, nodes, width), f32),
            pltpu.VMEM((WINDOW, nodes, width), f32),
        ],
        compiler_params=pltpu.CompilerParams(vmem_limit_bytes=40 * 2**20),
        cost_estimate=pl.CostEstimate(flops=6_000_000_000, bytes_accessed=5_000_000, transcendentals=0),
        name="filter",
    )(place, wavefunctions, *field_got, high, low)

    all_states = lax.all_gather(filtered, "band", axis=1, tiled=True)
    term = pl.pallas_call(
        margin_kernel,
        out_shape=jax.ShapeDtypeStruct((state_order.shape[0], width), f32),
        in_specs=[SMEM, VMEM, VMEM],
        out_specs=VMEM,
        compiler_params=pltpu.CompilerParams(vmem_limit_bytes=40 * 2**20),
        name="margin",
    )(place, all_states, state_order[None, :])
    rows = state_order.shape[0] // doms
    parts = lax.all_to_all(term.reshape(doms, rows, width), "dom", 0, 0, tiled=True)
    return (filtered, parts.sum(0) * (1.0 / (nodes * doms)))


def solution(mesh):
    in_specs = (P("dom", "band"), P("dom"), P("dom"), P(None, "dom"), P("dom"), P())
    out_specs = (P("dom", "band"), P("dom", "band"))
    return jax.shard_map(shards, mesh=mesh, in_specs=in_specs, out_specs=out_specs, check_vma=False)
```

time: 1040 us -> 83.7 us (0.08)
  waiting for transfers between devices: 762 us -> 0.02 us
  other arithmetic: 116 us -> 2.11 us
  local copies, waits for them, and re-layouts: 59.5 us -> 0.73 us
  starting transfers between devices: 55.4 us -> 16.8 us
  blocking collectives: 6.51 us -> 43.2 us
  Pallas kernels: 0 us -> 19.6 us
  matrix products: 15.5 us -> 0 us
  between operations: 15.5 us -> 0.76 us
    psum x1 -> x0, waiting for transfers between devices: 714 us -> none  [shards(): summed = lax.psum(term_part, 'dom')]
    scatter-add x16 -> x0, other arithmetic: 109 us -> none  [the longest x8 101 us: accumulate(): result.at[links.reshape(-1)].add(contrib.reshape(-1, contrib.shape[2]))]
    gather x17 -> x0, local copies, waits for them, and re-layouts: 50.7 us -> none  [the longest x8 43.7 us: contributions(): gathered = source[links.reshape(-1)].reshape(8, cell_count * state_width)]
    ppermute x16 -> x8, waiting for transfers between devices: 47.9 us -> 0.02 us  [swapped(): return lax.ppermute(block, axis, route)]
    ppermute x16 -> x8, starting transfers between devices: 55.4 us -> 16.8 us  [swapped(): return lax.ppermute(block, axis, route)]
    all_to_all x0 -> x1, blocking collectives: none -> 36.5 us  [shards(): lax.all_to_all(term.reshape(doms, rows, width), 'dom', 0, 0, tiled=True)]
    pallas_call x0 -> x3, Pallas kernels: none -> 19.6 us  [the longest x1 10.9 us: shards(): pl.pallas_call(build_kernel, out_shape=[jax.ShapeDtypeStruct((WINDOW, nod...]
    dot_general x9 -> x0, matrix products: 15.5 us -> none  [the longest x8 14.2 us: contributions(): jnp.dot(cell_table, gathered, precision=lax.Precision.HIGHEST, preferred_...]
  transfers between devices with their start and end apart: 17 -> 8, of which waited for: 17 -> 0; matrix products, arithmetic and copies ran while one was open for 0% -> 0% of each run, Pallas kernels for 0% -> 13%
where the time goes in v1:
time: 83.7 us; the launch traced here: 83.2 us
  blocking collectives  43.2 us (52%)
  Pallas kernels  19.6 us (23%)
  starting transfers between devices  16.8 us (20%)
  other arithmetic  2.11 us (3%)
    all_to_all x1, blocking collectives, shards(): lax.all_to_all(term.reshape(doms, rows, width), 'dom', 0, 0, tiled=True)  36.5 us
    ppermute x8, starting transfers between devices, swapped(): return lax.ppermute(block, axis, route)  16.8 us
    pallas_call x1, Pallas kernels, shards(): pl.pallas_call(build_kernel, out_shape=[jax.ShapeDtypeStruct((WINDOW, nod...  10.9 us
    pallas_call x1, Pallas kernels, shards(): pl.pallas_call(filter_kernel, out_shape=jax.ShapeDtypeStruct((nodes, widt...  7.14 us
    all_gather x1, blocking collectives, shards(): all_states = lax.all_gather(filtered, 'band', axis=1, tiled=True)  6.71 us
  transfers between devices with their start and end apart: 8, of which 0 were waited for; matrix products, arithmetic and copies ran while one was open for 0% of the time, Pallas kernels for 13%

profile of v1, /device:TPU:32, one launch (start us, length us, event | category | flops | bytes accessed | tf_op | source)
XLA Modules:
  0.0 83.2 jit_solution(10920326518045564451)
XLA Ops:
  0.6 0.7 convert_element_type.7
  1.3 0.7 convert_element_type.6
  2.0 0.7 concatenate.3.own
  2.7 0.7 collective-permute-start.7
  3.4 5.8 %collective-permute-start.6 = (f32[16,256]{1,0:T(8,128)S(1)}, f32[16,256]{1,0:T(8,128)S(1)}, u32[]{:S(2)}, u32[]{:S(2)}) collective-permute-start(f32[16,256]{1,0:T(8,128)S(1)} %concatenate.3.own), channel_id=1, source_target_pairs={{0,8},{8,0},{4,12},{12,4},{16,24},{24,16},{20,28},{28,20},{32,40},... | collective-permute-start | bytes 49160 | tf_op jit(solution)/shard_map/ppermute | solution.py:207
  9.2 0.7 collective-permute-start.5
  9.8 2.9 %collective-permute-start.4 = (f32[16,256]{1,0:T(8,128)S(1)}, f32[16,256]{1,0:T(8,128)S(1)}, u32[]{:S(2)}, u32[]{:S(2)}) collective-permute-start(f32[16,256]{1,0:T(8,128)S(1)} %concatenate.3.own), channel_id=1, source_target_pairs={{0,4},{4,0},{8,12},{12,8},{16,20},{20,16},{24,28},{28,24},{32,36},... | collective-permute-start | bytes 49160 | tf_op jit(solution)/shard_map/ppermute | solution.py:207
  12.7 4.0 %collective-permute-start.2 = (f32[256,128]{1,0:T(8,128)}, f32[256,128]{1,0:T(8,128)S(1)}, u32[]{:S(2)}, u32[]{:S(2)}) collective-permute-start(f32[256,128]{1,0:T(8,128)} %own.1), channel_id=1, source_target_pairs={{0,8},{8,0},{4,12},{12,4},{16,24},{24,16},{20,28},{28,20},{32,40},... | collective-permute-start | bytes 393224 | tf_op jit(solution)/shard_map/ppermute | solution.py:207
  16.8 0.1 pad_add_fusion.place
  16.9 0.0 collective-permute-done.7
  16.9 0.7 collective-permute-start.1
  17.5 1.3 %collective-permute-start = (f32[256,128]{1,0:T(8,128)}, f32[256,128]{1,0:T(8,128)S(1)}, u32[]{:S(2)}, u32[]{:S(2)}) collective-permute-start(f32[256,128]{1,0:T(8,128)} %own.1), channel_id=1, source_target_pairs={{0,4},{4,0},{8,12},{12,8},{16,20},{20,16},{24,28},{28,24},{32,36},... | collective-permute-start | bytes 393224 | tf_op jit(solution)/shard_map/ppermute | solution.py:207
  18.8 0.8 %collective-permute-start.3 = (f32[256,128]{1,0:T(8,128)}, f32[256,128]{1,0:T(8,128)S(1)}, u32[]{:S(2)}, u32[]{:S(2)}) collective-permute-start(f32[256,128]{1,0:T(8,128)} %own.1), channel_id=1, source_target_pairs={{8,16},{16,8},{12,20},{20,12},{24,32},{32,24},{28,36},{36,28},{40,... | collective-permute-start | bytes 393224 | tf_op jit(solution)/shard_map/ppermute | solution.py:207
  19.7 0.0 copy-start.1
  19.7 10.9 %build.1 = (bf16[5,256,768]{2,1,0:T(8,128)(2,1)S(1)}, bf16[5,256,768]{2,1,0:T(8,128)(2,1)S(1)}) custom-call(s32[3]{0:T(128)S(1)} %pad_add_fusion.place, f32[16,256]{1,0:T(8,128)S(1)} %concatenate.3.own, f32[16,256]{1,0:T(8,128)S(1)} %get-tuple-element.9.r1, f32[16,256]{1,0:T(8,128)S(1)} %get-tuple-element.8.l1, f32[16,256]{1,0:T(8,128)S(1)} %get-tuple-element.7.r2, ...), custom_call_target="tpu_custom_call" | custom-call | flops 8000000000 | bytes 4000000 | tf_op jit(solution)/shard_map/build/pallas_call | solution.py:244
  30.6 0.0 collective-permute-done.1.near_b
  30.6 0.0 collective-permute-done.near_a
  30.6 0.0 copy-start
  30.7 7.1 %filter.1 = f32[256,128]{1,0:T(8,128)} custom-call(s32[3]{0:T(128)S(1)} %pad_add_fusion.place, f32[256,128]{1,0:T(8,128)S(1)} %copy-done.1, f32[256,128]{1,0:T(8,128)S(1)} %collective-permute-done.near_a, f32[256,128]{1,0:T(8,128)S(1)} %collective-permute-done.1.near_b, f32[256,128]{1,0:T(8,128)S(1)} %collective-permute-done.2.far_a, ...), custom_call_target="tpu_custom_call" | custom-call | flops 6000000000 | bytes 5000000 | tf_op jit(solution)/shard_map/filter/pallas_call | solution.py:255
  37.8 6.7 %all_gather.3.states = f32[256,512]{1,0:T(8,128)S(1)} all-gather(f32[256,128]{1,0:T(8,128)} %filter.1), channel_id=1, replica_groups=mesh['dom'=64,'band'=4] {'band'}, dimensions={1}, use_global_device_ids=true | all-gather | bytes 655360 | tf_op jit(solution)/shard_map/all_gather | solution.py:271
  44.5 1.6 %margin.1 = f32[512,128]{1,0:T(8,128)S(1)} custom-call(s32[3]{0:T(128)S(1)} %pad_add_fusion.place, f32[256,512]{1,0:T(8,128)S(1)} %all_gather.3.states, s32[1,512]{1,0:T(1,128)S(1)} %bitcast.8), custom_call_target="tpu_custom_call" | custom-call | tf_op jit(solution)/shard_map/margin/pallas_call | solution.py:272
  46.1 36.5 %all_to_all.5 = f32[64,8,128]{2,1,0:T(8,128)S(1)} all-to-all(f32[64,8,128]{2,1,0:T(8,128)S(1)} %bitcast.7), channel_id=1, replica_groups=mesh['dom'=64,'band'=4] {'dom'}, dimensions={0} | all-to-all | bytes 524288 | tf_op jit(solution)/shard_map/all_to_all | solution.py:281
  82.6 0.1 reduce_sum.9
  82.6 0.6 broadcast_multiply_fusion
  (11 shorter events, 0.0 us)
Async XLA Ops:
  2.7 14.1 %collective-permute-start.7 = (f32[16,256]{1,0:T(8,128)S(1)}, f32[16,256]{1,0:T(8,128)S(1)}, u32[]{:S(2)}, u32[]{:S(2)}) collective-permute-start(f32[16,256]{1,0:T(8,128)S(1)} %concatenate.3.own), channel_id=1, source_target_pairs={{8,16},{16,8},{12,20},{20,12},{24,32},{32,24},{28,36},{36,28},{40,... | collective-permute-start | bytes 49160 | tf_op jit(solution)/shard_map/ppermute | solution.py:207
  3.4 14.2 %collective-permute-start.6 = (f32[16,256]{1,0:T(8,128)S(1)}, f32[16,256]{1,0:T(8,128)S(1)}, u32[]{:S(2)}, u32[]{:S(2)}) collective-permute-start(f32[16,256]{1,0:T(8,128)S(1)} %concatenate.3.own), channel_id=1, source_target_pairs={{0,8},{8,0},{4,12},{12,4},{16,24},{24,16},{20,28},{28,20},{32,40},... | collective-permute-start | bytes 49160 | tf_op jit(solution)/shard_map/ppermute | solution.py:207
  9.2 9.7 %collective-permute-start.5 = (f32[16,256]{1,0:T(8,128)S(1)}, f32[16,256]{1,0:T(8,128)S(1)}, u32[]{:S(2)}, u32[]{:S(2)}) collective-permute-start(f32[16,256]{1,0:T(8,128)S(1)} %concatenate.3.own), channel_id=1, source_target_pairs={{4,8},{8,4},{12,16},{16,12},{20,24},{24,20},{28,32},{32,28},{36,40... | collective-permute-start | bytes 49160 | tf_op jit(solution)/shard_map/ppermute | solution.py:207
  9.8 9.9 %collective-permute-start.4 = (f32[16,256]{1,0:T(8,128)S(1)}, f32[16,256]{1,0:T(8,128)S(1)}, u32[]{:S(2)}, u32[]{:S(2)}) collective-permute-start(f32[16,256]{1,0:T(8,128)S(1)} %concatenate.3.own), channel_id=1, source_target_pairs={{0,4},{4,0},{8,12},{12,8},{16,20},{20,16},{24,28},{28,24},{32,36},... | collective-permute-start | bytes 49160 | tf_op jit(solution)/shard_map/ppermute | solution.py:207
  12.7 17.9 %collective-permute-start.2 = (f32[256,128]{1,0:T(8,128)}, f32[256,128]{1,0:T(8,128)S(1)}, u32[]{:S(2)}, u32[]{:S(2)}) collective-permute-start(f32[256,128]{1,0:T(8,128)} %own.1), channel_id=1, source_target_pairs={{0,8},{8,0},{4,12},{12,4},{16,24},{24,16},{20,28},{28,20},{32,40},... | collective-permute-start | bytes 393224 | tf_op jit(solution)/shard_map/ppermute | solution.py:207
  16.9 13.8 %collective-permute-start.1 = (f32[256,128]{1,0:T(8,128)}, f32[256,128]{1,0:T(8,128)S(1)}, u32[]{:S(2)}, u32[]{:S(2)}) collective-permute-start(f32[256,128]{1,0:T(8,128)} %own.1), channel_id=1, source_target_pairs={{4,8},{8,4},{12,16},{16,12},{20,24},{24,20},{28,32},{32,28},{36,40... | collective-permute-start | bytes 393224 | tf_op jit(solution)/shard_map/ppermute | solution.py:207
  17.5 13.1 %collective-permute-start = (f32[256,128]{1,0:T(8,128)}, f32[256,128]{1,0:T(8,128)S(1)}, u32[]{:S(2)}, u32[]{:S(2)}) collective-permute-start(f32[256,128]{1,0:T(8,128)} %own.1), channel_id=1, source_target_pairs={{0,4},{4,0},{8,12},{12,8},{16,20},{20,16},{24,28},{28,24},{32,36},... | collective-permute-start | bytes 393224 | tf_op jit(solution)/shard_map/ppermute | solution.py:207
  18.8 11.8 %collective-permute-start.3 = (f32[256,128]{1,0:T(8,128)}, f32[256,128]{1,0:T(8,128)S(1)}, u32[]{:S(2)}, u32[]{:S(2)}) collective-permute-start(f32[256,128]{1,0:T(8,128)} %own.1), channel_id=1, source_target_pairs={{8,16},{16,8},{12,20},{20,12},{24,32},{32,24},{28,36},{36,28},{40,... | collective-permute-start | bytes 393224 | tf_op jit(solution)/shard_map/ppermute | solution.py:207
  19.7 10.9 %copy-start.1 = (f32[256,128]{1,0:T(8,128)S(1)}, f32[256,128]{1,0:T(8,128)}, u32[]{:S(2)}) copy-start(f32[256,128]{1,0:T(8,128)} %own.1) | copy-start | bytes 393220
  30.6 13.9 %copy-start = (s32[512]{0:T(512)S(1)}, s32[512]{0:T(512)}, u32[]{:S(2)}) copy-start(s32[512]{0:T(512)} %param.11) | copy-start | bytes 6148

commit v2 on v0

v2 whole, which is shorter than its diff:
```python
import jax
import jax.numpy as jnp
import numpy as np
from jax import lax
from jax.experimental import pallas as pl
from jax.experimental.pallas import tpu as pltpu
from jax.sharding import PartitionSpec as P

DEGREE = 8
REACH = 2
WINDOW = 2 * REACH + 1
LAYERS = 4
EXTRA = 24

lower_cut = 1.5
upper_edge = 5.0
anchor_value = 0.4

half_span = (upper_edge - lower_cut) / 2.0
center = (upper_edge + lower_cut) / 2.0
sigma_first = half_span / (anchor_value - center)
gamma_value = 2.0 / sigma_first


VMEM = pl.BlockSpec(memory_space=pltpu.VMEM)
SMEM = pl.BlockSpec(memory_space=pltpu.SMEM)
ANY = pl.BlockSpec(memory_space=pl.ANY)
f32 = jnp.float32
bf16 = jnp.bfloat16


def dot(a, b):
    return lax.dot_general(a, b, (((1,), (0,)), ((), ())), preferred_element_type=f32)


def dot_t(a, b):
    return lax.dot_general(a, b, (((1,), (1,)), ((), ())), preferred_element_type=f32)


def split(x):
    high = x.astype(bf16)
    return high, (x - high.astype(f32)).astype(bf16)


def coarse_parts(x):
    parts = []
    for _ in range(3):
        scaled = x * float(2**19 + 1)
        part = scaled - (scaled - x)
        parts.append(part)
        x = x - part
    return parts


def exact(x):
    high, rest = x.astype(bf16), x
    terms = [high]
    for _ in range(2):
        rest = rest - terms[-1].astype(f32)
        terms.append(rest.astype(bf16))
    return terms


def cross(a, b):
    return lax.dot_general(a, b, (((0,), (0,)), ((), ())), preferred_element_type=f32)


def iota(shape, dim):
    return lax.broadcasted_iota(jnp.int32, shape, dim)


def flag(mask):
    return jnp.where(mask, 1.0, 0.0).astype(bf16)


def column_of(row):
    count = row.shape[1]
    terms = jnp.concatenate([t.astype(f32) for t in exact(row)] + [jnp.zeros((13, count), f32)], 0)
    return cross(terms.astype(bf16), jnp.ones((16, 128), bf16))


def sort_kernel(field, links, potential, mass, plane, out, rank_out, field_in, links_in, rows_in, plane_in, sems):
    nodes, width = field.shape
    copies = [
        pltpu.make_async_copy(field, field_in, sems.at[0]),
        pltpu.make_async_copy(links, links_in, sems.at[1]),
        pltpu.make_async_copy(potential, rows_in.at[pl.ds(0, 1)], sems.at[2]),
        pltpu.make_async_copy(mass, rows_in.at[pl.ds(1, 1)], sems.at[3]),
        pltpu.make_async_copy(plane, plane_in, sems.at[4]),
    ]
    for copy in copies:
        copy.start()
    for copy in copies[1:]:
        copy.wait()
    corners = links_in[...]
    corner_id = corners.astype(f32)
    plane_count = plane.shape[1]
    plane_row = jnp.concatenate([plane_in[...].astype(f32), jnp.full((1, 128 - plane_count), -1.0, f32)], 1)

    row_id = iota((nodes, nodes), 0).astype(f32)
    lane_id = iota((nodes, nodes), 1).astype(f32)
    row_small = row_id.astype(bf16)
    touched = None
    for a in range(8):
        hits = jnp.where(row_small == corner_id[a : a + 1, :].astype(bf16), jnp.ones_like(row_small), jnp.zeros_like(row_small))
        touched = hits if touched is None else touched + hits
    span = nodes // LAYERS
    by_layer = flag(iota((nodes, 128 * LAYERS), 0) // span == iota((nodes, 128 * LAYERS), 1) // 128)
    counts = dot(touched, by_layer)
    layer = [counts[:, 128 * i : 128 * (i + 1)] > 0.5 for i in range(LAYERS)]
    in_plane = flag(row_id[:, :128] == plane_row)
    is_plane = dot(in_plane, jnp.ones((128, 128), bf16)) > 0.5
    least = jnp.where(layer[0], 0.0, jnp.where(layer[1], 1.0, jnp.where(layer[2], 2.0, 3.0)))
    most = jnp.where(layer[3], 3.0, jnp.where(layer[2], 2.0, jnp.where(layer[1], 1.0, 0.0)))
    key = jnp.where(is_plane, -1.0, least + most)
    key_row = cross(key.astype(bf16), flag(row_id == lane_id))[0:1, :]
    order_col = key * float(nodes) + row_id[:, :128]
    order_row = key_row * float(nodes) + lane_id[0:1, :]
    before = flag(jnp.concatenate([order_col] * (nodes // 128), 1) < order_row)
    counted = dot(jnp.ones((16, nodes), bf16), before)[0:1, :]
    sub = iota((16, 128), 0)
    plane_facts = dot_t(
        jnp.where(sub == 0, 1.0, jnp.where(sub == 1, iota((16, 128), 1).astype(f32), 0.0)).astype(bf16), in_plane
    )
    rank = jnp.where(plane_facts[0:1, :] > 0.5, plane_facts[1:2, :], counted)
    rank_out[...] = jnp.broadcast_to(rank, rank_out.shape)

    low_lane = iota((8, 128), 1) < 64
    ranks = [jnp.broadcast_to(rank[:, 128 * h : 128 * (h + 1)], (8, 128)) for h in range(2)]
    for m in range(2):
        part = corners[:, 128 * m : 128 * (m + 1)]
        local = lax.bitwise_and(part, 127)
        found = [jnp.take_along_axis(r, local, axis=1) for r in ranks]
        place = jnp.where(part < 128, found[0], jnp.where(part < nodes, found[1], part.astype(f32)))
        place = place - jnp.where(low_lane, 128.0 * m, 128.0 * m + 64.0)
        turned = pltpu.roll(place, 64, 1)
        chance = rows_in[0:1, 128 * m : 128 * (m + 1)]
        chance = jnp.broadcast_to(chance, (8, 128))
        chance_turned = pltpu.roll(chance, 64, 1)
        for i in range(4):
            even, odd = slice(2 * i, 2 * i + 1), slice(2 * i + 1, 2 * i + 2)
            at = nodes + 8 * m + i
            out[at : at + 1, :] = jnp.where(low_lane[0:1], place[even], turned[odd])
            out[at + 4 : at + 5, :] = jnp.where(low_lane[0:1], turned[even], place[odd])
        at = nodes + 16 + 2 * m
        out[at : at + 1, :] = jnp.where(low_lane, chance, chance_turned)[0:1]
        out[at + 1 : at + 2, :] = jnp.where(low_lane, chance_turned, chance)[0:1]

    move = flag(row_id == rank)
    scale = lax.rsqrt(rows_in[1:2, :])
    terms = jnp.concatenate([t.astype(f32) for t in exact(scale)] + [jnp.zeros((13, nodes), f32)], 0)
    moved = dot_t(terms.astype(bf16), move)
    scale = moved[0:1] + moved[1:2] + moved[2:3]
    out[nodes + 20 : nodes + 21, :] = scale[:, :128]
    out[nodes + 21 : nodes + 22, :] = scale[:, 128:]
    out[nodes + 22 : nodes + 24, :] = jnp.zeros((2, 128), f32)
    copies[0].wait()
    sorted_field = dot(move, jnp.concatenate(exact(field_in[...]), 1))
    sorted_field = sorted_field[:, :width] + sorted_field[:, width : 2 * width] + sorted_field[:, 2 * width :]
    out[:nodes, :] = sorted_field * column_of(scale)


def layer_matrix(table, layer, scratch):
    plain, pair, third = scratch
    low_lane = iota((1, 128), 1) < 64
    chance = table[16 + layer : 17 + layer, :]
    stiff = (0.0, 1.0 / 2.0, 1.0 / 3.0, 1.0 / 6.0)
    mass = (1.0 / 8.0, 1.0 / 24.0, 1.0 / 72.0, 1.0 / 216.0)
    whole = [(0.5 * k + chance * m) * 0.125 for k, m in zip(stiff, mass)]

    def spread(row):
        return jnp.broadcast_to(row, (16, 128)).astype(bf16)

    weights = [
        [spread(part) for part in coarse_parts(jnp.where(low_lane, whole[j], whole[j + 1]))] for j in range(3)
    ]
    rows = table[4 * layer : 4 * layer + 4, :]
    turned = pltpu.roll(table[8 * (layer // 2) : 8 * (layer // 2) + 8, :], 64, 1)
    turned = turned[4 * (layer % 2) : 4 * (layer % 2) + 4, :]
    straight = [spread(rows[i : i + 1, :]) for i in range(4)]
    opposite = [spread(turned[i : i + 1, :]) for i in range(4)]
    sign = spread(jnp.where(low_lane, 1.0, -1.0))
    one, zero = jnp.ones((16, 128), bf16), jnp.zeros((16, 128), bf16)
    for r in range(8):
        local = (iota((16, 128), 0) + 16 * r).astype(f32).astype(bf16)
        items = [
            jnp.where(local == s, sign, zero) + jnp.where(local == o, one, zero) for s, o in zip(straight, opposite)
        ]
        for bit in (1, 2):
            mixed = [None] * 4
            for i in range(4):
                if not i & bit:
                    mixed[i] = items[i] + items[i | bit]
                    mixed[i | bit] = items[i] - items[i | bit]
            items = mixed
        for i in range(4):
            part = weights[bin(i).count("1")]
            lanes = slice(128 * i, 128 * (i + 1))
            plain[16 * r : 16 * r + 16, lanes] = items[i]
            pair[16 * r : 16 * r + 16, lanes] = items[i] * part[0]
            pair[128 + 16 * r : 128 + 16 * r + 16, lanes] = items[i] * part[1]
            third[16 * r : 16 * r + 16, lanes] = items[i] * part[2]
    both = dot_t(plain[...], pair[...])
    return both[:, :128] + both[:, 128:] + dot_t(plain[...], third[...])


def partition_matrices(table, scratch, layers, out, first):
    for layer in layers:
        out[first + layer] = layer_matrix(table, layer, [ref.at[layer] for ref in scratch])


def own_kernel(packed, out, *scratch):
    partition_matrices(packed[packed.shape[0] - EXTRA :, :], scratch, range(LAYERS), out, 0)


def sides(choose, got_a, got_b, part):
    a, b = got_a[part, :], got_b[part, :]
    return jnp.where(choose, b, a), jnp.where(choose, a, b)


def near_kernel(place, got_a, got_b, out, *scratch):
    is_even = lax.rem(place[0], 2) == 0
    nodes = got_a.shape[0] - EXTRA
    for i, table in enumerate(sides(is_even, got_a, got_b, slice(nodes, nodes + EXTRA))):
        partition_matrices(table, scratch, range(LAYERS), out, LAYERS * i)


def filter_kernel(place, packed, near_a, near_b, far_a, far_b, rank_ref, own_cells, near_cells,
                  out, far_cells, bands, even, odd, field_a, field_b, *scratch):
    position = place[0]
    nodes, width = out.shape
    span = nodes // LAYERS
    table_part, field_part = slice(nodes, nodes + EXTRA), slice(0, nodes)
    is_even = lax.rem(position, 2) == 0
    is_low = lax.rem(position, 4) < 2
    left1, right1 = sides(is_even, near_a, near_b, table_part)
    left2, right2 = sides(is_low, far_a, far_b, table_part)
    tables = (left2, left1, packed[table_part, :], right1, right2)
    partition_matrices(left2, scratch, range(LAYERS), far_cells, 0)
    partition_matrices(right2, scratch, range(LAYERS - 1), far_cells, LAYERS)
    cells = [far_cells[i] for i in range(4)] + [near_cells[i] for i in range(4)] + [own_cells[i] for i in range(4)]
    cells += [near_cells[4 + i] for i in range(4)] + [far_cells[4 + i] for i in range(3)] + [None]

    low_lane = iota((128, 128), 1) < span
    on_first = iota((128, 128), 1) == iota((128, 128), 0) + span
    on_second = iota((128, 128), 1) == iota((128, 128), 0) - span
    blank = jnp.zeros((span, 128), f32)
    pairs = len(cells) // 2
    for q in range(WINDOW):
        scale = column_of(jnp.concatenate([tables[q][20:21], tables[q][21:22]], 1))
        weight = scale * scale * (1.0 / half_span)
        for j in (2 * q, 2 * q + 1):
            rows = slice(128 * (j - 2 * q), 128 * (j - 2 * q) + 128)
            turned = pltpu.roll(cells[2 * j], 64, 1)
            upper = blank if j == 0 else cells[2 * j - 1][span:, :]
            lower = blank if cells[2 * j + 1] is None else cells[2 * j + 1][:span, :]
            first = jnp.concatenate([upper, blank], 0) + jnp.where(low_lane, 0.0, turned)
            second = jnp.concatenate([blank, lower], 0) + jnp.where(low_lane, turned, 0.0)
            first = first * weight[rows, :] - jnp.where(on_first, center / half_span, 0.0)
            second = second * weight[rows, :] - jnp.where(on_second, center / half_span, 0.0)
            for lanes, value in ((slice(0, 128), first), (slice(128, 256), second)):
                high, low = split(value)
                bands[j, :128, lanes] = high
                bands[j, 128:, lanes] = low

    def put(target, at, value):
        count = value.shape[0]
        high, low = split(value)
        target[span + at : span + at + count, :width] = high
        target[span + at : span + at + count, width:] = low

    for target in (even, odd):
        target[:span, :] = jnp.zeros((span, 2 * width), bf16)
        target[span + WINDOW * nodes :, :] = jnp.zeros((span, 2 * width), bf16)
    field1 = sides(is_even, near_a, near_b, field_part)
    field2 = sides(is_low, far_a, far_b, field_part)
    for q, value in enumerate((field2[0], field1[0], packed[field_part, :], field1[1], field2[1])):
        field_a[nodes * q : nodes * (q + 1), :] = value
        put(even, nodes * q, value)
    sigma_last = sigma_first
    final = []
    for k in range(1, DEGREE + 1):
        source, target = (even, odd) if k % 2 else (odd, even)
        newer = field_b if k % 2 else field_a
        if k == 1:
            gain, keep = sigma_first, None
        else:
            sigma_next = 1.0 / (gamma_value - sigma_last)
            gain, keep = 2.0 * sigma_next, sigma_last * sigma_next
            sigma_last = sigma_next
        for j in range(k // 2, pairs - k // 2):
            product = dot(bands[j], source[128 * j : 128 * j + 256, :])
            value = gain * (product[:128, :width] + (product[:128, width:] + product[128:, :width]))
            if keep is not None:
                value = value - keep * newer[128 * j : 128 * (j + 1), :]
            if k == DEGREE:
                final.append(value)
            else:
                newer[128 * j : 128 * (j + 1), :] = value
                put(target, 128 * j, value)
    scale = column_of(jnp.concatenate([tables[REACH][20:21], tables[REACH][21:22]], 1))
    result = jnp.concatenate(final, 0) / scale
    move = flag(iota((nodes, nodes), 0).astype(f32) == rank_ref[0:1, :])
    back = cross(move, jnp.concatenate(exact(result), 1))
    out[...] = back[:, :width] + back[:, width : 2 * width] + back[:, 2 * width :]


def margin_kernel(place, states, order, out):
    band = place[1]
    count = order.shape[1]
    width = out.shape[1]
    state_id = lax.broadcasted_iota(jnp.int32, (count, count), 0)
    pick = jnp.where(state_id == order[...], 1.0, 0.0).astype(bf16)
    high, low = split(states[...])
    high = dot(high, pick)
    low = dot(low, pick).astype(bf16)
    high = high.astype(bf16)
    own_order = order[:, pl.ds(pl.multiple_of(band * width, width), width)]
    own_pick = jnp.where(state_id[:, :width] == own_order, 1.0, 0.0).astype(bf16)
    own_high, own_low = split(states[...])
    own_high = dot(own_high, own_pick).astype(bf16)
    own_low = dot(own_low, own_pick).astype(bf16)

    def cross(a, b):
        return lax.dot_general(a, b, (((0,), (0,)), ((), ())), preferred_element_type=f32)

    out[...] = cross(high, own_high) + cross(high, own_low) + cross(low, own_high)


def swapped(block, axis, pairs):
    count = lax.axis_size(axis)
    route = [
        step for a, b in pairs if a < count and b < count for step in ((a, b), (b, a))
    ]
    return lax.ppermute(block, axis, route)


def shards(wavefunctions, node_mass, cell_potential, cell_nodes, plane_nodes, state_order):
    nodes, width = wavefunctions.shape
    doms = lax.axis_size("dom")
    place = jnp.stack([lax.axis_index("dom"), lax.axis_index("band")]).astype(jnp.int32)
    near_pairs = [
        [(2 * i, 2 * i + 1) for i in range(doms)],
        [(2 * i + 1, 2 * i + 2) for i in range(doms)],
    ]
    far_pairs = [
        [(4 * i + j, 4 * i + j + 2) for i in range(doms) for j in range(2)],
        [(4 * i + j + 2, 4 * i + j + 4) for i in range(doms) for j in range(2)],
    ]
    params = pltpu.CompilerParams(vmem_limit_bytes=40 * 2**20)
    plane_count = plane_nodes.shape[0]

    packed, rank = pl.pallas_call(
        sort_kernel,
        out_shape=[jax.ShapeDtypeStruct((nodes + EXTRA, width), f32), jax.ShapeDtypeStruct((8, nodes), f32)],
        in_specs=[ANY] * 5,
        out_specs=[VMEM] * 2,
        scratch_shapes=[
            pltpu.VMEM((nodes, width), f32),
            pltpu.VMEM((8, nodes), jnp.int32),
            pltpu.VMEM((2, nodes), f32),
            pltpu.VMEM((1, plane_count), jnp.int32),
            pltpu.SemaphoreType.DMA((5,)),
        ],
        compiler_params=pltpu.CompilerParams(vmem_limit_bytes=60 * 2**20),
        name="sort",
    )(wavefunctions, cell_nodes, cell_potential[None, :], node_mass[None, :], plane_nodes[None, :])
    near_b, far_b, near_a, far_a = [
        swapped(packed, "dom", pairs)
        for pairs in (near_pairs[1], far_pairs[1], near_pairs[0], far_pairs[0])
    ]
    incidence = [
        pltpu.VMEM((LAYERS, 128, 512), bf16),
        pltpu.VMEM((LAYERS, 256, 512), bf16),
        pltpu.VMEM((LAYERS, 128, 512), bf16),
    ]
    own_cells = pl.pallas_call(
        own_kernel,
        out_shape=jax.ShapeDtypeStruct((LAYERS, 128, 128), f32),
        in_specs=[VMEM],
        out_specs=VMEM,
        scratch_shapes=incidence,
        compiler_params=params,
        cost_estimate=pl.CostEstimate(flops=1_000_000_000, bytes_accessed=1_000_000, transcendentals=0),
        name="own",
    )(packed)
    near_cells = pl.pallas_call(
        near_kernel,
        out_shape=jax.ShapeDtypeStruct((2 * LAYERS, 128, 128), f32),
        in_specs=[SMEM] + [VMEM] * 2,
        out_specs=VMEM,
        scratch_shapes=incidence,
        compiler_params=params,
        cost_estimate=pl.CostEstimate(flops=2_000_000_000, bytes_accessed=1_000_000, transcendentals=0),
        name="near",
    )(place, near_a, near_b)
    padded = (WINDOW + 1) * nodes - (nodes - 2 * (nodes // LAYERS))
    filtered = pl.pallas_call(
        filter_kernel,
        out_shape=jax.ShapeDtypeStruct((nodes, width), f32),
        in_specs=[SMEM] + [VMEM] * 8,
        out_specs=VMEM,
        scratch_shapes=[
            pltpu.VMEM((2 * LAYERS, 128, 128), f32),
            pltpu.VMEM((WINDOW * LAYERS // 2, 256, 256), bf16),
            pltpu.VMEM((padded, 2 * width), bf16),
            pltpu.VMEM((padded, 2 * width), bf16),
            pltpu.VMEM((WINDOW * nodes, width), f32),
            pltpu.VMEM((WINDOW * nodes, width), f32),
        ]
        + incidence,
        compiler_params=params,
        name="filter",
    )(place, packed, near_a, near_b, far_a, far_b, rank, own_cells, near_cells)

    all_states = lax.all_gather(filtered, "band", axis=1, tiled=True)
    term = pl.pallas_call(
        margin_kernel,
        out_shape=jax.ShapeDtypeStruct((state_order.shape[0], width), f32),
        in_specs=[SMEM, VMEM, VMEM],
        out_specs=VMEM,
        compiler_params=pltpu.CompilerParams(vmem_limit_bytes=40 * 2**20),
        name="margin",
    )(place, all_states, state_order[None, :])
    rows = state_order.shape[0] // doms
    parts = lax.all_to_all(term.reshape(doms, rows, width), "dom", 0, 0, tiled=True)
    return (filtered, parts.sum(0) * (1.0 / (nodes * doms)))


def solution(mesh):
    in_specs = (P("dom", "band"), P("dom"), P("dom"), P(None, "dom"), P("dom"), P())
    out_specs = (P("dom", "band"), P("dom", "band"))
    return jax.shard_map(shards, mesh=mesh, in_specs=in_specs, out_specs=out_specs, check_vma=False)
```

time: 1040 us -> 70.7 us (0.07)
  waiting for transfers between devices: 762 us -> 6.11 us
  other arithmetic: 116 us -> 0.74 us
  local copies, waits for them, and re-layouts: 59.5 us -> 0.95 us
  starting transfers between devices: 55.4 us -> 10 us
  blocking collectives: 6.51 us -> 39.9 us
  matrix products: 15.5 us -> 0 us
  between operations: 15.5 us -> 0.72 us
  Pallas kernels: 0 us -> 12 us
    psum x1 -> x0, waiting for transfers between devices: 714 us -> none  [shards(): summed = lax.psum(term_part, 'dom')]
    scatter-add x16 -> x0, other arithmetic: 109 us -> none  [the longest x8 101 us: accumulate(): result.at[links.reshape(-1)].add(contrib.reshape(-1, contrib.shape[2]))]
    gather x17 -> x0, local copies, waits for them, and re-layouts: 50.7 us -> none  [the longest x8 43.7 us: contributions(): gathered = source[links.reshape(-1)].reshape(8, cell_count * state_width)]
    ppermute x16 -> x4, starting transfers between devices: 55.4 us -> 10 us  [swapped(): return lax.ppermute(block, axis, route)]
    ppermute x16 -> x4, waiting for transfers between devices: 47.9 us -> 6.11 us  [swapped(): return lax.ppermute(block, axis, route)]
    all_to_all x0 -> x1, blocking collectives: none -> 32.6 us  [shards(): lax.all_to_all(term.reshape(doms, rows, width), 'dom', 0, 0, tiled=True)]
    dot_general x9 -> x0, matrix products: 15.5 us -> none  [the longest x8 14.2 us: contributions(): jnp.dot(cell_table, gathered, precision=lax.Precision.HIGHEST, preferred_...]
    pallas_call x0 -> x5, Pallas kernels: none -> 12 us  [the longest x1 5.32 us: shards(): pl.pallas_call(filter_kernel, out_shape=jax.ShapeDtypeStruct((nodes, widt...]
  transfers between devices with their start and end apart: 17 -> 4, of which waited for: 17 -> 1; matrix products, arithmetic and copies ran while one was open for 0% -> 0% of each run, Pallas kernels for 0% -> 4%
where the time goes in v2:
time: 70.7 us; the launch traced here: 70.4 us
  blocking collectives  39.9 us (56%)
  Pallas kernels  12 us (17%)
  starting transfers between devices  10 us (14%)
  waiting for transfers between devices  6.11 us (9%)
  local copies, waits for them, and re-layouts  0.95 us (1%)
  other arithmetic  0.74 us (1%)
  between operations  0.72 us (1%)
    all_to_all x1, blocking collectives, shards(): lax.all_to_all(term.reshape(doms, rows, width), 'dom', 0, 0, tiled=True)  32.6 us
    ppermute x4, starting transfers between devices, swapped(): return lax.ppermute(block, axis, route)  10 us
    all_gather x1, blocking collectives, shards(): all_states = lax.all_gather(filtered, 'band', axis=1, tiled=True)  7.29 us
    ppermute x4, waiting for transfers between devices, swapped(): return lax.ppermute(block, axis, route)  6.11 us
    pallas_call x1, Pallas kernels, shards(): pl.pallas_call(filter_kernel, out_shape=jax.ShapeDtypeStruct((nodes, widt...  5.32 us
    pallas_call x1, Pallas kernels, shards(): pl.pallas_call(sort_kernel, out_shape=[jax.ShapeDtypeStruct((nodes + EXTR...  2.56 us
    pallas_call x1, Pallas kernels, shards(): pl.pallas_call(near_kernel, out_shape=jax.ShapeDtypeStruct((2 * LAYERS, 1...  1.83 us
    pallas_call x1, Pallas kernels, shards(): pl.pallas_call(margin_kernel, out_shape=jax.ShapeDtypeStruct((state_order...  1.56 us
  transfers between devices with their start and end apart: 4, of which 1 were waited for; matrix products, arithmetic and copies ran while one was open for 0% of the time, Pallas kernels for 4%

profile of v2, /device:TPU:32, one launch (start us, length us, event | category | flops | bytes accessed | tf_op | source)
XLA Modules:
  0.0 70.4 jit_solution(14007814958460746528)
XLA Ops:
  0.6 2.6 %sort.1 = (f32[280,128]{1,0:T(8,128)}, f32[8,256]{1,0:T(8,128)}) custom-call(f32[256,128]{1,0:T(8,128)} %field.1, s32[8,256]{1,0:T(8,128)} %links.1, f32[1,256]{1,0:T(1,128)} %bitcast.9, f32[1,256]{1,0:T(1,128)} %bitcast.10, s32[1,64]{1,0:T(1,128)} %bitcast.11), custom_call_target="tpu_custom_call" | custom-call | tf_op jit(solution)/shard_map/sort/pallas_call | solution.py:353
  3.2 0.7 collective-permute-start.3
  3.9 5.8 %collective-permute-start.2 = (f32[280,128]{1,0:T(8,128)}, f32[280,128]{1,0:T(8,128)S(1)}, u32[]{:S(2)}, u32[]{:S(2)}) collective-permute-start(f32[280,128]{1,0:T(8,128)} %get-tuple-element.4.packed), channel_id=1, source_target_pairs={{0,8},{8,0},{4,12},{12,4},{16,24},{24,16},{20,28},{28,20},{32,40},... | collective-permute-start | bytes 430088 | tf_op jit(solution)/shard_map/ppermute | solution.py:335
  9.7 0.7 collective-permute-start.1
  10.3 2.9 %collective-permute-start = (f32[280,128]{1,0:T(8,128)}, f32[280,128]{1,0:T(8,128)S(1)}, u32[]{:S(2)}, u32[]{:S(2)}) collective-permute-start(f32[280,128]{1,0:T(8,128)} %get-tuple-element.4.packed), channel_id=1, source_target_pairs={{0,4},{4,0},{8,12},{12,8},{16,20},{20,16},{24,28},{28,24},{32,36},... | collective-permute-start | bytes 430088 | tf_op jit(solution)/shard_map/ppermute | solution.py:335
  13.2 0.9 %copy-done = f32[280,128]{1,0:T(8,128)S(1)} copy-done((f32[280,128]{1,0:T(8,128)S(1)}, f32[280,128]{1,0:T(8,128)}, u32[]{:S(2)}) %copy-start) | copy-done | bytes 143384
  14.2 0.7 %own.1.own_cells = f32[4,128,128]{2,1,0:T(8,128)S(1)} custom-call(f32[280,128]{1,0:T(8,128)S(1)} %copy-done), custom_call_target="tpu_custom_call" | custom-call | flops 1000000000 | bytes 1000000 | tf_op jit(solution)/shard_map/own/pallas_call | solution.py:377
  14.9 0.1 pad_add_fusion.place
  15.0 0.0 copy-start.1
  15.0 0.0 copy-start.2
  15.0 0.0 collective-permute-done.1.got_b.near_b
  15.0 6.1 %collective-permute-done.got_a.near_a = f32[280,128]{1,0:T(8,128)S(1)} collective-permute-done((f32[280,128]{1,0:T(8,128)}, f32[280,128]{1,0:T(8,128)S(1)}, u32[]{:S(2)}, u32[]{:S(2)}) %collective-permute-start) | collective-permute-done | bytes 143392 | tf_op jit(solution)/shard_map/ppermute | solution.py:335
  21.1 1.8 %near.1.near_cells = f32[8,128,128]{2,1,0:T(8,128)S(1)} custom-call(s32[2]{0:T(128)S(1)} %pad_add_fusion.place, f32[280,128]{1,0:T(8,128)S(1)} %collective-permute-done.got_a.near_a, f32[280,128]{1,0:T(8,128)S(1)} %collective-permute-done.1.got_b.near_b), custom_call_target="tpu_custom_call" | custom-call | flops 2000000000 | bytes 1000000 | tf_op jit(solution)/shard_map/near/pallas_call | solution.py:387
  23.0 0.0 collective-permute-done.3.far_b
  23.0 0.0 collective-permute-done.2.far_a
  23.0 0.0 copy-done.1
  23.0 0.0 copy-done.2
  23.0 5.3 %filter.1 = f32[256,128]{1,0:T(8,128)} custom-call(s32[2]{0:T(128)S(1)} %pad_add_fusion.place, f32[280,128]{1,0:T(8,128)S(1)} %copy-done.1, f32[280,128]{1,0:T(8,128)S(1)} %collective-permute-done.got_a.near_a, f32[280,128]{1,0:T(8,128)S(1)} %collective-permute-done.1.got_b.near_b, f32[280,128]{1,0:T(8,128)S(1)} %collective-permute-done.2.far_a, ...), custom_call_target="tpu_custom_call" | custom-call | tf_op jit(solution)/shard_map/filter/pallas_call | solution.py:398
  28.3 7.3 %all_gather.3.states = f32[256,512]{1,0:T(8,128)S(1)} all-gather(f32[256,128]{1,0:T(8,128)} %filter.1), channel_id=1, replica_groups=mesh['dom'=64,'band'=4] {'band'}, dimensions={1}, use_global_device_ids=true | all-gather | bytes 655360 | tf_op jit(solution)/shard_map/all_gather | solution.py:416
  35.6 0.0 copy-done.3
  35.6 1.6 %margin.1 = f32[512,128]{1,0:T(8,128)S(1)} custom-call(s32[2]{0:T(128)S(1)} %pad_add_fusion.place, f32[256,512]{1,0:T(8,128)S(1)} %all_gather.3.states, s32[1,512]{1,0:T(1,128)S(1)} %bitcast.8), custom_call_target="tpu_custom_call" | custom-call | tf_op jit(solution)/shard_map/margin/pallas_call | solution.py:417
  37.2 32.6 %all_to_all.5 = f32[64,8,128]{2,1,0:T(8,128)S(1)} all-to-all(f32[64,8,128]{2,1,0:T(8,128)S(1)} %bitcast.7), channel_id=1, replica_groups=mesh['dom'=64,'band'=4] {'dom'}, dimensions={0} | all-to-all | bytes 524288 | tf_op jit(solution)/shard_map/all_to_all | solution.py:426
  69.8 0.1 reduce_sum.9
  69.8 0.6 broadcast_multiply_fusion
  (2 shorter events, 0.0 us)
Async XLA Ops:
  3.2 19.8 %collective-permute-start.3 = (f32[280,128]{1,0:T(8,128)}, f32[280,128]{1,0:T(8,128)S(1)}, u32[]{:S(2)}, u32[]{:S(2)}) collective-permute-start(f32[280,128]{1,0:T(8,128)} %get-tuple-element.4.packed), channel_id=1, source_target_pairs={{8,16},{16,8},{12,20},{20,12},{24,32},{32,24},{28,36},{36,28},{40,... | collective-permute-start | bytes 430088 | tf_op jit(solution)/shard_map/ppermute | solution.py:335
  3.9 19.1 %collective-permute-start.2 = (f32[280,128]{1,0:T(8,128)}, f32[280,128]{1,0:T(8,128)S(1)}, u32[]{:S(2)}, u32[]{:S(2)}) collective-permute-start(f32[280,128]{1,0:T(8,128)} %get-tuple-element.4.packed), channel_id=1, source_target_pairs={{0,8},{8,0},{4,12},{12,4},{16,24},{24,16},{20,28},{28,20},{32,40},... | collective-permute-start | bytes 430088 | tf_op jit(solution)/shard_map/ppermute | solution.py:335
  9.7 5.4 %collective-permute-start.1 = (f32[280,128]{1,0:T(8,128)}, f32[280,128]{1,0:T(8,128)S(1)}, u32[]{:S(2)}, u32[]{:S(2)}) collective-permute-start(f32[280,128]{1,0:T(8,128)} %get-tuple-element.4.packed), channel_id=1, source_target_pairs={{4,8},{8,4},{12,16},{16,12},{20,24},{24,20},{28,32},{32,28},{36,40... | collective-permute-start | bytes 430088 | tf_op jit(solution)/shard_map/ppermute | solution.py:335
  10.3 10.8 %collective-permute-start = (f32[280,128]{1,0:T(8,128)}, f32[280,128]{1,0:T(8,128)S(1)}, u32[]{:S(2)}, u32[]{:S(2)}) collective-permute-start(f32[280,128]{1,0:T(8,128)} %get-tuple-element.4.packed), channel_id=1, source_target_pairs={{0,4},{4,0},{8,12},{12,8},{16,20},{20,16},{24,28},{28,24},{32,36},... | collective-permute-start | bytes 430088 | tf_op jit(solution)/shard_map/ppermute | solution.py:335
  13.2 0.9 %copy-start = (f32[280,128]{1,0:T(8,128)S(1)}, f32[280,128]{1,0:T(8,128)}, u32[]{:S(2)}) copy-start(f32[280,128]{1,0:T(8,128)} %get-tuple-element.4.packed) | copy-start | bytes 430084
  15.0 8.0 %copy-start.1 = (f32[280,128]{1,0:T(8,128)S(1)}, f32[280,128]{1,0:T(8,128)}, u32[]{:S(2)}) copy-start(f32[280,128]{1,0:T(8,128)} %get-tuple-element.4.packed) | copy-start | bytes 430084
  15.0 8.0 %copy-start.2 = (f32[8,256]{1,0:T(8,128)S(1)}, f32[8,256]{1,0:T(8,128)}, u32[]{:S(2)}) copy-start(f32[8,256]{1,0:T(8,128)} %get-tuple-element.5.rank_ref) | copy-start | bytes 24580
  28.3 7.3 %copy-start.3 = (s32[512]{0:T(512)S(1)}, s32[512]{0:T(512)}, u32[]{:S(2)}) copy-start(s32[512]{0:T(512)} %param.11) | copy-start | bytes 6148

commit v3 on v2

--- a/solution.py
+++ b/solution.py
@@ -113,15 +113,19 @@
     least = jnp.where(layer[0], 0.0, jnp.where(layer[1], 1.0, jnp.where(layer[2], 2.0, 3.0)))
     most = jnp.where(layer[3], 3.0, jnp.where(layer[2], 2.0, jnp.where(layer[1], 1.0, 0.0)))
     key = jnp.where(is_plane, -1.0, least + most)
-    key_row = cross(key.astype(bf16), flag(row_id == lane_id))[0:1, :]
+    sub = iota((16, 128), 0)
+    plane_facts = dot_t(
+        jnp.where(sub == 0, 1.0, jnp.where(sub == 1, iota((16, 128), 1).astype(f32), 0.0)).astype(bf16), in_plane
+    )
+    row_counts = dot_t(flag(iota((16, nodes), 0) == iota((16, nodes), 1) // span), touched)
+    row_layer = [row_counts[i : i + 1, :] > 0.5 for i in range(LAYERS)]
+    row_least = jnp.where(row_layer[0], 0.0, jnp.where(row_layer[1], 1.0, jnp.where(row_layer[2], 2.0, 3.0)))
+    row_most = jnp.where(row_layer[3], 3.0, jnp.where(row_layer[2], 2.0, jnp.where(row_layer[1], 1.0, 0.0)))
+    key_row = jnp.where(plane_facts[0:1, :] > 0.5, -1.0, row_least + row_most)
     order_col = key * float(nodes) + row_id[:, :128]
     order_row = key_row * float(nodes) + lane_id[0:1, :]
     before = flag(jnp.concatenate([order_col] * (nodes // 128), 1) < order_row)
     counted = dot(jnp.ones((16, nodes), bf16), before)[0:1, :]
-    sub = iota((16, 128), 0)
-    plane_facts = dot_t(
-        jnp.where(sub == 0, 1.0, jnp.where(sub == 1, iota((16, 128), 1).astype(f32), 0.0)).astype(bf16), in_plane
-    )
     rank = jnp.where(plane_facts[0:1, :] > 0.5, plane_facts[1:2, :], counted)
     rank_out[...] = jnp.broadcast_to(rank, rank_out.shape)
 
@@ -209,37 +213,54 @@
         out[first + layer] = layer_matrix(table, layer, [ref.at[layer] for ref in scratch])
 
 
-def own_kernel(packed, out, *scratch):
+def own_kernel(packed, rank, out, back, *scratch):
+    nodes = back.shape[0]
+    place = jnp.concatenate([column_of(rank[0:1, :])] * (nodes // 128), 1)
+    back[...] = flag(place == iota((nodes, nodes), 1).astype(f32))
     partition_matrices(packed[packed.shape[0] - EXTRA :, :], scratch, range(LAYERS), out, 0)
 
 
-def sides(choose, got_a, got_b, part):
-    a, b = got_a[part, :], got_b[part, :]
-    return jnp.where(choose, b, a), jnp.where(choose, a, b)
-
-
-def near_kernel(place, got_a, got_b, out, *scratch):
+def around(place, inner, outer, relay_a, relay_b):
+    in_four = lax.rem(place[0], 4)
     is_even = lax.rem(place[0], 2) == 0
-    nodes = got_a.shape[0] - EXTRA
-    for i, table in enumerate(sides(is_even, got_a, got_b, slice(nodes, nodes + EXTRA))):
+    left1 = jnp.where(is_even, outer, inner)
+    right1 = jnp.where(is_even, inner, outer)
+    left2 = jnp.where(in_four < 2, relay_b, relay_a)
+    right2 = jnp.where(in_four < 2, relay_a, relay_b)
+    return left2, left1, right1, right2
+
+
+def outer_of(place, got_a, got_b, part):
+    in_four = lax.rem(place[0], 4)
+    by_b = jnp.logical_or(in_four == 0, in_four == 3)
+    return jnp.where(by_b, got_b[part, :], got_a[part, :])
+
+
+def near_kernel(place, inner, got_a, got_b, relay_a, out, *scratch):
+    nodes = inner.shape[0] - EXTRA
+    part = slice(nodes, nodes + EXTRA)
+    for i, table in enumerate((inner[part, :], outer_of(place, got_a, got_b, part), relay_a[part, :])):
         partition_matrices(table, scratch, range(LAYERS), out, LAYERS * i)
 
 
-def filter_kernel(place, packed, near_a, near_b, far_a, far_b, rank_ref, own_cells, near_cells,
+def filter_kernel(place, packed, inner, got_a, got_b, relay_a, relay_b, back, own_cells, near_cells,
                   out, far_cells, bands, even, odd, field_a, field_b, *scratch):
-    position = place[0]
     nodes, width = out.shape
     span = nodes // LAYERS
     table_part, field_part = slice(nodes, nodes + EXTRA), slice(0, nodes)
-    is_even = lax.rem(position, 2) == 0
-    is_low = lax.rem(position, 4) < 2
-    left1, right1 = sides(is_even, near_a, near_b, table_part)
-    left2, right2 = sides(is_low, far_a, far_b, table_part)
-    tables = (left2, left1, packed[table_part, :], right1, right2)
-    partition_matrices(left2, scratch, range(LAYERS), far_cells, 0)
-    partition_matrices(right2, scratch, range(LAYERS - 1), far_cells, LAYERS)
-    cells = [far_cells[i] for i in range(4)] + [near_cells[i] for i in range(4)] + [own_cells[i] for i in range(4)]
-    cells += [near_cells[4 + i] for i in range(4)] + [far_cells[4 + i] for i in range(3)] + [None]
+    last = relay_b[table_part, :]
+    partition_matrices(last, scratch, range(LAYERS), far_cells, 0)
+
+    def window(part):
+        sides = around(place, inner[part, :], outer_of(place, got_a, got_b, part), relay_a[part, :], relay_b[part, :])
+        return sides[:2] + (packed[part, :],) + sides[2:]
+
+    tables = window(table_part)
+    cells = []
+    for i in range(LAYERS):
+        cells.append(around(place, near_cells[i], near_cells[LAYERS + i], near_cells[2 * LAYERS + i], far_cells[i]))
+    cells = [cells[i][0] for i in range(4)] + [cells[i][1] for i in range(4)] + [own_cells[i] for i in range(4)] + [
+        cells[i][2] for i in range(4)] + [cells[i][3] for i in range(3)] + [None]
 
     low_lane = iota((128, 128), 1) < span
     on_first = iota((128, 128), 1) == iota((128, 128), 0) + span
@@ -272,9 +293,7 @@
     for target in (even, odd):
         target[:span, :] = jnp.zeros((span, 2 * width), bf16)
         target[span + WINDOW * nodes :, :] = jnp.zeros((span, 2 * width), bf16)
-    field1 = sides(is_even, near_a, near_b, field_part)
-    field2 = sides(is_low, far_a, far_b, field_part)
-    for q, value in enumerate((field2[0], field1[0], packed[field_part, :], field1[1], field2[1])):
+    for q, value in enumerate(window(field_part)):
         field_a[nodes * q : nodes * (q + 1), :] = value
         put(even, nodes * q, value)
     sigma_last = sigma_first
@@ -299,10 +318,8 @@
                 newer[128 * j : 128 * (j + 1), :] = value
                 put(target, 128 * j, value)
     scale = column_of(jnp.concatenate([tables[REACH][20:21], tables[REACH][21:22]], 1))
-    result = jnp.concatenate(final, 0) / scale
-    move = flag(iota((nodes, nodes), 0).astype(f32) == rank_ref[0:1, :])
-    back = cross(move, jnp.concatenate(exact(result), 1))
-    out[...] = back[:, :width] + back[:, width : 2 * width] + back[:, 2 * width :]
+    moved = dot(back[...], jnp.concatenate(exact(jnp.concatenate(final, 0) / scale), 1))
+    out[...] = moved[:, :width] + moved[:, width : 2 * width] + moved[:, 2 * width :]
 
 
 def margin_kernel(place, states, order, out):
@@ -330,7 +347,7 @@
 def swapped(block, axis, pairs):
     count = lax.axis_size(axis)
     route = [
-        step for a, b in pairs if a < count and b < count for step in ((a, b), (b, a))
+        step for a, b in pairs if 0 <= a and b < count for step in ((a, b), (b, a))
     ]
     return lax.ppermute(block, axis, route)
 
@@ -339,14 +356,10 @@
     nodes, width = wavefunctions.shape
     doms = lax.axis_size("dom")
     place = jnp.stack([lax.axis_index("dom"), lax.axis_index("band")]).astype(jnp.int32)
-    near_pairs = [
-        [(2 * i, 2 * i + 1) for i in range(doms)],
-        [(2 * i + 1, 2 * i + 2) for i in range(doms)],
-    ]
-    far_pairs = [
-        [(4 * i + j, 4 * i + j + 2) for i in range(doms) for j in range(2)],
-        [(4 * i + j + 2, 4 * i + j + 4) for i in range(doms) for j in range(2)],
-    ]
+    pairs = [(2 * i, 2 * i + 1) for i in range(doms)]
+    fours = range(-1, doms // 4 + 1)
+    mirror_a = [(4 * i + j, 4 * i + 3 - j) for i in fours for j in (0, 1)]
+    mirror_b = [(4 * i + 2 + j, 4 * i + 5 - j) for i in fours for j in (0, 1)]
     params = pltpu.CompilerParams(vmem_limit_bytes=40 * 2**20)
     plane_count = plane_nodes.shape[0]
 
@@ -365,43 +378,41 @@
         compiler_params=pltpu.CompilerParams(vmem_limit_bytes=60 * 2**20),
         name="sort",
     )(wavefunctions, cell_nodes, cell_potential[None, :], node_mass[None, :], plane_nodes[None, :])
-    near_b, far_b, near_a, far_a = [
-        swapped(packed, "dom", pairs)
-        for pairs in (near_pairs[1], far_pairs[1], near_pairs[0], far_pairs[0])
-    ]
+    got_b, got_a, inner = [swapped(packed, "dom", route) for route in (mirror_b, mirror_a, pairs)]
+    relay_a, relay_b = [swapped(block, "dom", pairs) for block in (got_a, got_b)]
     incidence = [
         pltpu.VMEM((LAYERS, 128, 512), bf16),
         pltpu.VMEM((LAYERS, 256, 512), bf16),
         pltpu.VMEM((LAYERS, 128, 512), bf16),
     ]
-    own_cells = pl.pallas_call(
+    own_cells, back = pl.pallas_call(
         own_kernel,
-        out_shape=jax.ShapeDtypeStruct((LAYERS, 128, 128), f32),
-        in_specs=[VMEM],
-        out_specs=VMEM,
+        out_shape=[jax.ShapeDtypeStruct((LAYERS, 128, 128), f32), jax.ShapeDtypeStruct((nodes, nodes), bf16)],
+        in_specs=[VMEM] * 2,
+        out_specs=[VMEM] * 2,
         scratch_shapes=incidence,
         compiler_params=params,
         cost_estimate=pl.CostEstimate(flops=1_000_000_000, bytes_accessed=1_000_000, transcendentals=0),
         name="own",
-    )(packed)
+    )(packed, rank)
     near_cells = pl.pallas_call(
         near_kernel,
-        out_shape=jax.ShapeDtypeStruct((2 * LAYERS, 128, 128), f32),
-        in_specs=[SMEM] + [VMEM] * 2,
+        out_shape=jax.ShapeDtypeStruct((3 * LAYERS, 128, 128), f32),
+        in_specs=[SMEM] + [VMEM] * 4,
         out_specs=VMEM,
         scratch_shapes=incidence,
         compiler_params=params,
         cost_estimate=pl.CostEstimate(flops=2_000_000_000, bytes_accessed=1_000_000, transcendentals=0),
         name="near",
-    )(place, near_a, near_b)
+    )(place, inner, got_a, got_b, relay_a)
     padded = (WINDOW + 1) * nodes - (nodes - 2 * (nodes // LAYERS))
     filtered = pl.pallas_call(
         filter_kernel,
         out_shape=jax.ShapeDtypeStruct((nodes, width), f32),
-        in_specs=[SMEM] + [VMEM] * 8,
+        in_specs=[SMEM] + [VMEM] * 9,
         out_specs=VMEM,
         scratch_shapes=[
-            pltpu.VMEM((2 * LAYERS, 128, 128), f32),
+            pltpu.VMEM((LAYERS, 128, 128), f32),
             pltpu.VMEM((WINDOW * LAYERS // 2, 256, 256), bf16),
             pltpu.VMEM((padded, 2 * width), bf16),
             pltpu.VMEM((padded, 2 * width), bf16),
@@ -411,7 +422,7 @@
         + incidence,
         compiler_params=params,
         name="filter",
-    )(place, packed, near_a, near_b, far_a, far_b, rank, own_cells, near_cells)
+    )(place, packed, inner, got_a, got_b, relay_a, relay_b, back, own_cells, near_cells)
 
     all_states = lax.all_gather(filtered, "band", axis=1, tiled=True)
     term = pl.pallas_call(

time: 70.7 us -> 67.1 us (0.949)
  starting transfers between devices: 10 us -> 6.04 us
  waiting for transfers between devices: 6.11 us -> 5.08 us
  blocking collectives: 39.9 us -> 40.7 us
    ppermute x4 -> x5, starting transfers between devices: 10 us -> 6.04 us  [swapped(): return lax.ppermute(block, axis, route)]
    all_to_all x1, blocking collectives: 32.6 us -> 33.9 us  [shards(): lax.all_to_all(term.reshape(doms, rows, width), 'dom', 0, 0, tiled=True)]
    ppermute x4 -> x5, waiting for transfers between devices: 6.11 us -> 5.08 us  [swapped(): return lax.ppermute(block, axis, route)]
  transfers between devices with their start and end apart: 4 -> 5, of which waited for: 1 -> 2; matrix products, arithmetic and copies ran while one was open for 0% -> 0% of each run, Pallas kernels for 4% -> 5%
where the time goes in v3:
time: 67.1 us; the launch traced here: 66.9 us
  blocking collectives  40.7 us (61%)
  Pallas kernels  12 us (18%)
  starting transfers between devices  6.04 us (9%)
  waiting for transfers between devices  5.08 us (8%)
  local copies, waits for them, and re-layouts  1.61 us (2%)
  other arithmetic  0.74 us (1%)
  between operations  0.69 us (1%)
    all_to_all x1, blocking collectives, shards(): lax.all_to_all(term.reshape(doms, rows, width), 'dom', 0, 0, tiled=True)  33.9 us
    all_gather x1, blocking collectives, shards(): all_states = lax.all_gather(filtered, 'band', axis=1, tiled=True)  6.84 us
    ppermute x5, starting transfers between devices, swapped(): return lax.ppermute(block, axis, route)  6.04 us
    ppermute x5, waiting for transfers between devices, swapped(): return lax.ppermute(block, axis, route)  5.08 us
    pallas_call x1, Pallas kernels, shards(): pl.pallas_call(filter_kernel, out_shape=jax.ShapeDtypeStruct((nodes, widt...  4.88 us
    pallas_call x1, Pallas kernels, shards(): pl.pallas_call(sort_kernel, out_shape=[jax.ShapeDtypeStruct((nodes + EXTR...  2.43 us
    pallas_call x1, Pallas kernels, shards(): pl.pallas_call(near_kernel, out_shape=jax.ShapeDtypeStruct((3 * LAYERS, 1...  2.37 us
    unnamed x8, local copies, waits for them, and re-layouts  1.61 us
  transfers between devices with their start and end apart: 5, of which 2 were waited for; matrix products, arithmetic and copies ran while one was open for 0% of the time, Pallas kernels for 5%

profile of v3, /device:TPU:32, one launch (start us, length us, event | category | flops | bytes accessed | tf_op | source)
XLA Modules:
  0.0 66.9 jit_solution(16654740401584222273)
XLA Ops:
  0.6 2.4 %sort.1 = (f32[280,128]{1,0:T(8,128)}, f32[8,256]{1,0:T(8,128)}) custom-call(f32[256,128]{1,0:T(8,128)} %field.1, s32[8,256]{1,0:T(8,128)} %links.1, f32[1,256]{1,0:T(1,128)} %bitcast.9, f32[1,256]{1,0:T(1,128)} %bitcast.10, s32[1,64]{1,0:T(1,128)} %bitcast.11), custom_call_target="tpu_custom_call" | custom-call | tf_op jit(solution)/shard_map/sort/pallas_call | solution.py:366
  3.1 3.1 %collective-permute-start.1 = (f32[280,128]{1,0:T(8,128)}, f32[280,128]{1,0:T(8,128)S(1)}, u32[]{:S(2)}, u32[]{:S(2)}) collective-permute-start(f32[280,128]{1,0:T(8,128)} %get-tuple-element.6.packed), channel_id=1, source_target_pairs={{0,12},{12,0},{4,8},{8,4},{16,28},{28,16},{20,24},{24,20},{32,44},... | collective-permute-start | bytes 430088 | tf_op jit(solution)/shard_map/ppermute | solution.py:352
  6.2 0.7 collective-permute-start.2
  6.8 0.2 collective-permute-start
  7.1 3.1 %collective-permute-done.1.got_a = f32[280,128]{1,0:T(8,128)S(1)} collective-permute-done((f32[280,128]{1,0:T(8,128)}, f32[280,128]{1,0:T(8,128)S(1)}, u32[]{:S(2)}, u32[]{:S(2)}) %collective-permute-start.1) | collective-permute-done | bytes 143392 | tf_op jit(solution)/shard_map/ppermute | solution.py:352
  10.1 0.3 collective-permute-start.3
  10.4 0.9 %copy-done = f32[280,128]{1,0:T(8,128)S(1)} copy-done((f32[280,128]{1,0:T(8,128)S(1)}, f32[280,128]{1,0:T(8,128)}, u32[]{:S(2)}) %copy-start) | copy-done | bytes 143384
  11.3 0.7 %copy-done.3 = f32[8,256]{1,0:T(8,128)S(1)} copy-done((f32[8,256]{1,0:T(8,128)S(1)}, f32[8,256]{1,0:T(8,128)}, u32[]{:S(2)}) %copy-start.3) | copy-done | bytes 8216
  12.0 0.8 %own.1 = (f32[4,128,128]{2,1,0:T(8,128)S(1)}, bf16[256,256]{1,0:T(8,128)(2,1)S(1)}) custom-call(f32[280,128]{1,0:T(8,128)S(1)} %copy-done, f32[8,256]{1,0:T(8,128)S(1)} %copy-done.3), custom_call_target="tpu_custom_call" | custom-call | flops 1000000000 | bytes 1000000 | tf_op jit(solution)/shard_map/own/pallas_call | solution.py:388
  12.8 0.1 pad_add_fusion.place
  12.9 0.0 collective-permute-done.2.got_b
  12.9 1.8 %collective-permute-start.4 = (f32[280,128]{1,0:T(8,128)S(1)}, f32[280,128]{1,0:T(8,128)S(1)}, u32[]{:S(2)}, u32[]{:S(2)}) collective-permute-start(f32[280,128]{1,0:T(8,128)S(1)} %collective-permute-done.2.got_b), channel_id=1, source_target_pairs={{0,4},{4,0},{8,12},{12,8},{16,20},{20,16},{24,28},{28,24},{32,36},... | collective-permute-start | bytes 430088 | tf_op jit(solution)/shard_map/ppermute | solution.py:352
  14.7 0.0 collective-permute-done.inner
  14.7 2.0 %collective-permute-done.3.relay_a = f32[280,128]{1,0:T(8,128)S(1)} collective-permute-done((f32[280,128]{1,0:T(8,128)S(1)}, f32[280,128]{1,0:T(8,128)S(1)}, u32[]{:S(2)}, u32[]{:S(2)}) %collective-permute-start.3) | collective-permute-done | bytes 143392 | tf_op jit(solution)/shard_map/ppermute | solution.py:352
  16.7 2.4 %near.1.near_cells = f32[12,128,128]{2,1,0:T(8,128)S(1)} custom-call(s32[2]{0:T(128)S(1)} %pad_add_fusion.place, f32[280,128]{1,0:T(8,128)S(1)} %collective-permute-done.inner, f32[280,128]{1,0:T(8,128)S(1)} %collective-permute-done.1.got_a, f32[280,128]{1,0:T(8,128)S(1)} %collective-permute-done.2.got_b, f32[280,128]{1,0:T(8,128)S(1)} %collective-permute-done.3.relay_a), custom_call_target="tpu_custom_call" | custom-call | flops 2000000000 | bytes 1000000 | tf_op jit(solution)/shard_map/near/pallas_call | solution.py:398
  19.0 0.0 collective-permute-done.4.relay_b
  19.0 0.0 copy-done.1
  19.1 4.9 %filter.1 = f32[256,128]{1,0:T(8,128)} custom-call(s32[2]{0:T(128)S(1)} %pad_add_fusion.place, f32[280,128]{1,0:T(8,128)S(1)} %copy-done.1, f32[280,128]{1,0:T(8,128)S(1)} %collective-permute-done.inner, f32[280,128]{1,0:T(8,128)S(1)} %collective-permute-done.1.got_a, f32[280,128]{1,0:T(8,128)S(1)} %collective-permute-done.2.got_b, ...), custom_call_target="tpu_custom_call" | custom-call | tf_op jit(solution)/shard_map/filter/pallas_call | solution.py:409
  23.9 6.8 %all_gather.3.states = f32[256,512]{1,0:T(8,128)S(1)} all-gather(f32[256,128]{1,0:T(8,128)} %filter.1), channel_id=1, replica_groups=mesh['dom'=64,'band'=4] {'band'}, dimensions={1}, use_global_device_ids=true | all-gather | bytes 655360 | tf_op jit(solution)/shard_map/all_gather | solution.py:427
  30.8 0.0 copy-done.2
  30.8 1.6 %margin.1 = f32[512,128]{1,0:T(8,128)S(1)} custom-call(s32[2]{0:T(128)S(1)} %pad_add_fusion.place, f32[256,512]{1,0:T(8,128)S(1)} %all_gather.3.states, s32[1,512]{1,0:T(1,128)S(1)} %bitcast.8), custom_call_target="tpu_custom_call" | custom-call | tf_op jit(solution)/shard_map/margin/pallas_call | solution.py:428
  32.3 33.9 %all_to_all.5 = f32[64,8,128]{2,1,0:T(8,128)S(1)} all-to-all(f32[64,8,128]{2,1,0:T(8,128)S(1)} %bitcast.7), channel_id=1, replica_groups=mesh['dom'=64,'band'=4] {'dom'}, dimensions={0} | all-to-all | bytes 524288 | tf_op jit(solution)/shard_map/all_to_all | solution.py:437
  66.2 0.1 reduce_sum.9
  66.3 0.6 broadcast_multiply_fusion
  (4 shorter events, 0.0 us)
Async XLA Ops:
  3.1 7.1 %collective-permute-start.1 = (f32[280,128]{1,0:T(8,128)}, f32[280,128]{1,0:T(8,128)S(1)}, u32[]{:S(2)}, u32[]{:S(2)}) collective-permute-start(f32[280,128]{1,0:T(8,128)} %get-tuple-element.6.packed), channel_id=1, source_target_pairs={{0,12},{12,0},{4,8},{8,4},{16,28},{28,16},{20,24},{24,20},{32,44},... | collective-permute-start | bytes 430088 | tf_op jit(solution)/shard_map/ppermute | solution.py:352
  6.2 6.7 %collective-permute-start.2 = (f32[280,128]{1,0:T(8,128)}, f32[280,128]{1,0:T(8,128)S(1)}, u32[]{:S(2)}, u32[]{:S(2)}) collective-permute-start(f32[280,128]{1,0:T(8,128)} %get-tuple-element.6.packed), channel_id=1, source_target_pairs={{8,20},{20,8},{12,16},{16,12},{24,36},{36,24},{28,32},{32,28},{40,... | collective-permute-start | bytes 430088 | tf_op jit(solution)/shard_map/ppermute | solution.py:352
  6.8 7.8 %collective-permute-start = (f32[280,128]{1,0:T(8,128)}, f32[280,128]{1,0:T(8,128)S(1)}, u32[]{:S(2)}, u32[]{:S(2)}) collective-permute-start(f32[280,128]{1,0:T(8,128)} %get-tuple-element.6.packed), channel_id=1, source_target_pairs={{0,4},{4,0},{8,12},{12,8},{16,20},{20,16},{24,28},{28,24},{32,36},... | collective-permute-start | bytes 430088 | tf_op jit(solution)/shard_map/ppermute | solution.py:352
  10.1 6.5 %collective-permute-start.3 = (f32[280,128]{1,0:T(8,128)S(1)}, f32[280,128]{1,0:T(8,128)S(1)}, u32[]{:S(2)}, u32[]{:S(2)}) collective-permute-start(f32[280,128]{1,0:T(8,128)S(1)} %collective-permute-done.1.got_a), channel_id=1, source_target_pairs={{0,4},{4,0},{8,12},{12,8},{16,20},{20,16},{24,28},{28,24},{32,36},... | collective-permute-start | bytes 430088 | tf_op jit(solution)/shard_map/ppermute | solution.py:352
  10.4 0.9 %copy-start = (f32[280,128]{1,0:T(8,128)S(1)}, f32[280,128]{1,0:T(8,128)}, u32[]{:S(2)}) copy-start(f32[280,128]{1,0:T(8,128)} %get-tuple-element.6.packed) | copy-start | bytes 430084
  11.3 0.7 %copy-start.3 = (f32[8,256]{1,0:T(8,128)S(1)}, f32[8,256]{1,0:T(8,128)}, u32[]{:S(2)}) copy-start(f32[8,256]{1,0:T(8,128)} %get-tuple-element.7.rank) | copy-start | bytes 24580
  12.9 6.2 %copy-start.1 = (f32[280,128]{1,0:T(8,128)S(1)}, f32[280,128]{1,0:T(8,128)}, u32[]{:S(2)}) copy-start(f32[280,128]{1,0:T(8,128)} %get-tuple-element.6.packed) | copy-start | bytes 430084
  12.9 6.1 %collective-permute-start.4 = (f32[280,128]{1,0:T(8,128)S(1)}, f32[280,128]{1,0:T(8,128)S(1)}, u32[]{:S(2)}, u32[]{:S(2)}) collective-permute-start(f32[280,128]{1,0:T(8,128)S(1)} %collective-permute-done.2.got_b), channel_id=1, source_target_pairs={{0,4},{4,0},{8,12},{12,8},{16,20},{20,16},{24,28},{28,24},{32,36},... | collective-permute-start | bytes 430088 | tf_op jit(solution)/shard_map/ppermute | solution.py:352
  23.9 6.8 %copy-start.2 = (s32[512]{0:T(512)S(1)}, s32[512]{0:T(512)}, u32[]{:S(2)}) copy-start(s32[512]{0:T(512)} %param.11) | copy-start | bytes 6148

commit v4 on v3

--- a/solution.py
+++ b/solution.py
@@ -213,8 +213,12 @@
         out[first + layer] = layer_matrix(table, layer, [ref.at[layer] for ref in scratch])
 
 
-def own_kernel(packed, rank, out, back, *scratch):
-    nodes = back.shape[0]
+def own_kernel(place, packed, rank, order, out, back, pick, own_pick, *scratch):
+    nodes, (count, width) = back.shape[0], own_pick.shape
+    state_id = iota((count, count), 0)
+    pick[...] = flag(state_id == order[...])
+    own_order = order[:, pl.ds(pl.multiple_of(place[1] * width, width), width)]
+    own_pick[...] = flag(state_id[:, :width] == own_order)
     place = jnp.concatenate([column_of(rank[0:1, :])] * (nodes // 128), 1)
     back[...] = flag(place == iota((nodes, nodes), 1).astype(f32))
     partition_matrices(packed[packed.shape[0] - EXTRA :, :], scratch, range(LAYERS), out, 0)
@@ -243,7 +247,7 @@
         partition_matrices(table, scratch, range(LAYERS), out, LAYERS * i)
 
 
-def filter_kernel(place, packed, inner, got_a, got_b, relay_a, relay_b, back, own_cells, near_cells,
+def filter_kernel(place, packed, inner, got_a, got_b, relay_a, relay_b, own_cells, near_cells,
                   out, far_cells, bands, even, odd, field_a, field_b, *scratch):
     nodes, width = out.shape
     span = nodes // LAYERS
@@ -318,30 +322,22 @@
                 newer[128 * j : 128 * (j + 1), :] = value
                 put(target, 128 * j, value)
     scale = column_of(jnp.concatenate([tables[REACH][20:21], tables[REACH][21:22]], 1))
-    moved = dot(back[...], jnp.concatenate(exact(jnp.concatenate(final, 0) / scale), 1))
-    out[...] = moved[:, :width] + moved[:, width : 2 * width] + moved[:, 2 * width :]
-
-
-def margin_kernel(place, states, order, out):
-    band = place[1]
-    count = order.shape[1]
+    out[...] = jnp.concatenate(final, 0) / scale
+
+
+def margin_kernel(states, pick, own_pick, own, back, out, filtered, original, sem):
     width = out.shape[1]
-    state_id = lax.broadcasted_iota(jnp.int32, (count, count), 0)
-    pick = jnp.where(state_id == order[...], 1.0, 0.0).astype(bf16)
+    moved = dot(back[...], jnp.concatenate(exact(own[...]), 1))
+    original[...] = moved[:, :width] + moved[:, width : 2 * width] + moved[:, 2 * width :]
+    copy = pltpu.make_async_copy(original, filtered, sem)
+    copy.start()
     high, low = split(states[...])
-    high = dot(high, pick)
-    low = dot(low, pick).astype(bf16)
-    high = high.astype(bf16)
-    own_order = order[:, pl.ds(pl.multiple_of(band * width, width), width)]
-    own_pick = jnp.where(state_id[:, :width] == own_order, 1.0, 0.0).astype(bf16)
-    own_high, own_low = split(states[...])
-    own_high = dot(own_high, own_pick).astype(bf16)
-    own_low = dot(own_low, own_pick).astype(bf16)
-
-    def cross(a, b):
-        return lax.dot_general(a, b, (((0,), (0,)), ((), ())), preferred_element_type=f32)
-
-    out[...] = cross(high, own_high) + cross(high, own_low) + cross(low, own_high)
+    own_high = dot(high, own_pick[...]).astype(bf16)
+    own_low = dot(low, own_pick[...]).astype(bf16)
+    part = cross(own_high, high) + cross(own_high, low) + cross(own_low, high)
+    chosen = [dot(term, pick[...]) for term in exact(part)]
+    out[...] = (chosen[0] + chosen[1] + chosen[2]).T
+    copy.wait()
 
 
 def swapped(block, axis, pairs):
@@ -385,16 +381,22 @@
         pltpu.VMEM((LAYERS, 256, 512), bf16),
         pltpu.VMEM((LAYERS, 128, 512), bf16),
     ]
-    own_cells, back = pl.pallas_call(
+    states = state_order.shape[0]
+    own_cells, back, pick, own_pick = pl.pallas_call(
         own_kernel,
-        out_shape=[jax.ShapeDtypeStruct((LAYERS, 128, 128), f32), jax.ShapeDtypeStruct((nodes, nodes), bf16)],
-        in_specs=[VMEM] * 2,
-        out_specs=[VMEM] * 2,
+        out_shape=[
+            jax.ShapeDtypeStruct((LAYERS, 128, 128), f32),
+            jax.ShapeDtypeStruct((nodes, nodes), bf16),
+            jax.ShapeDtypeStruct((states, states), bf16),
+            jax.ShapeDtypeStruct((states, width), bf16),
+        ],
+        in_specs=[SMEM] + [VMEM] * 3,
+        out_specs=[VMEM] * 4,
         scratch_shapes=incidence,
         compiler_params=params,
         cost_estimate=pl.CostEstimate(flops=1_000_000_000, bytes_accessed=1_000_000, transcendentals=0),
         name="own",
-    )(packed, rank)
+    )(place, packed, rank, state_order[None, :])
     near_cells = pl.pallas_call(
         near_kernel,
         out_shape=jax.ShapeDtypeStruct((3 * LAYERS, 128, 128), f32),
@@ -406,10 +408,10 @@
         name="near",
     )(place, inner, got_a, got_b, relay_a)
     padded = (WINDOW + 1) * nodes - (nodes - 2 * (nodes // LAYERS))
-    filtered = pl.pallas_call(
+    by_layer = pl.pallas_call(
         filter_kernel,
         out_shape=jax.ShapeDtypeStruct((nodes, width), f32),
-        in_specs=[SMEM] + [VMEM] * 9,
+        in_specs=[SMEM] + [VMEM] * 8,
         out_specs=VMEM,
         scratch_shapes=[
             pltpu.VMEM((LAYERS, 128, 128), f32),
@@ -422,17 +424,18 @@
         + incidence,
         compiler_params=params,
         name="filter",
-    )(place, packed, inner, got_a, got_b, relay_a, relay_b, back, own_cells, near_cells)
-
-    all_states = lax.all_gather(filtered, "band", axis=1, tiled=True)
-    term = pl.pallas_call(
+    )(place, packed, inner, got_a, got_b, relay_a, relay_b, own_cells, near_cells)
+
+    all_states = lax.all_gather(by_layer, "band", axis=1, tiled=True)
+    term, filtered = pl.pallas_call(
         margin_kernel,
-        out_shape=jax.ShapeDtypeStruct((state_order.shape[0], width), f32),
-        in_specs=[SMEM, VMEM, VMEM],
-        out_specs=VMEM,
-        compiler_params=pltpu.CompilerParams(vmem_limit_bytes=40 * 2**20),
+        out_shape=[jax.ShapeDtypeStruct((states, width), f32), jax.ShapeDtypeStruct((nodes, width), f32)],
+        in_specs=[VMEM] * 5,
+        out_specs=[VMEM, ANY],
+        scratch_shapes=[pltpu.VMEM((nodes, width), f32), pltpu.SemaphoreType.DMA],
+        compiler_params=params,
         name="margin",
-    )(place, all_states, state_order[None, :])
+    )(all_states, pick, own_pick, by_layer, back)
     rows = state_order.shape[0] // doms
     parts = lax.all_to_all(term.reshape(doms, rows, width), "dom", 0, 0, tiled=True)
     return (filtered, parts.sum(0) * (1.0 / (nodes * doms)))

time: 67.1 us -> 65.8 us (0.981)
  waiting for transfers between devices: 5.08 us -> 4.07 us
    ppermute x5, waiting for transfers between devices: 5.08 us -> 4.07 us  [swapped(): return lax.ppermute(block, axis, route)]
    pallas_call x1, Pallas kernels: 4.88 us -> 4.02 us  [shards(): pl.pallas_call(filter_kernel, out_shape=jax.ShapeDtypeStruct((nodes, widt...]
    pallas_call x1, Pallas kernels: 0.75 us -> 1.52 us  [shards(): pl.pallas_call(own_kernel, out_shape=[jax.ShapeDtypeStruct((LAYERS, 128,...]
  transfers between devices with their start and end apart: 5 -> 5, of which waited for: 2 -> 3; matrix products, arithmetic and copies ran while one was open for 0% -> 0% of each run, Pallas kernels for 5% -> 6%
where the time goes in v4:
time: 65.8 us; the launch traced here: 65.6 us
  blocking collectives  40.6 us (62%)
  Pallas kernels  11.8 us (18%)
  starting transfers between devices  6.09 us (9%)
  waiting for transfers between devices  4.07 us (6%)
  local copies, waits for them, and re-layouts  1.59 us (2%)
  other arithmetic  0.74 us (1%)
  between operations  0.7 us (1%)
    all_to_all x1, blocking collectives, shards(): lax.all_to_all(term.reshape(doms, rows, width), 'dom', 0, 0, tiled=True)  33.3 us
    all_gather x1, blocking collectives, shards(): all_states = lax.all_gather(by_layer, 'band', axis=1, tiled=True)  7.34 us
    ppermute x5, starting transfers between devices, swapped(): return lax.ppermute(block, axis, route)  6.09 us
    ppermute x5, waiting for transfers between devices, swapped(): return lax.ppermute(block, axis, route)  4.07 us
    pallas_call x1, Pallas kernels, shards(): pl.pallas_call(filter_kernel, out_shape=jax.ShapeDtypeStruct((nodes, widt...  4.02 us
    pallas_call x1, Pallas kernels, shards(): pl.pallas_call(sort_kernel, out_shape=[jax.ShapeDtypeStruct((nodes + EXTR...  2.43 us
    pallas_call x1, Pallas kernels, shards(): pl.pallas_call(near_kernel, out_shape=jax.ShapeDtypeStruct((3 * LAYERS, 1...  2.37 us
    unnamed x8, local copies, waits for them, and re-layouts  1.59 us
  transfers between devices with their start and end apart: 5, of which 3 were waited for; matrix products, arithmetic and copies ran while one was open for 0% of the time, Pallas kernels for 6%

profile of v4, /device:TPU:32, one launch (start us, length us, event | category | flops | bytes accessed | tf_op | source)
XLA Modules:
  0.0 65.6 jit_solution(5725235289145234312)
XLA Ops:
  0.6 2.4 %sort.1 = (f32[280,128]{1,0:T(8,128)}, f32[8,256]{1,0:T(8,128)}) custom-call(f32[256,128]{1,0:T(8,128)} %field.1, s32[8,256]{1,0:T(8,128)} %links.1, f32[1,256]{1,0:T(1,128)} %bitcast.9, f32[1,256]{1,0:T(1,128)} %bitcast.10, s32[1,64]{1,0:T(1,128)} %bitcast.11), custom_call_target="tpu_custom_call" | custom-call | tf_op jit(solution)/shard_map/sort/pallas_call | solution.py:362
  3.1 3.1 %collective-permute-start.1 = (f32[280,128]{1,0:T(8,128)}, f32[280,128]{1,0:T(8,128)S(1)}, u32[]{:S(2)}, u32[]{:S(2)}) collective-permute-start(f32[280,128]{1,0:T(8,128)} %get-tuple-element.10.packed), channel_id=1, source_target_pairs={{0,12},{12,0},{4,8},{8,4},{16,28},{28,16},{20,24},{24,20},{32,44},... | collective-permute-start | bytes 430088 | tf_op jit(solution)/shard_map/ppermute | solution.py:348
  6.2 0.7 %collective-permute-start.2 = (f32[280,128]{1,0:T(8,128)}, f32[280,128]{1,0:T(8,128)S(1)}, u32[]{:S(2)}, u32[]{:S(2)}) collective-permute-start(f32[280,128]{1,0:T(8,128)} %get-tuple-element.10.packed), channel_id=1, source_target_pairs={{8,20},{20,8},{12,16},{16,12},{24,36},{36,24},{28,32},{32,28},{40,... | collective-permute-start | bytes 430088 | tf_op jit(solution)/shard_map/ppermute | solution.py:348
  6.8 0.2 collective-permute-start
  7.1 3.1 %collective-permute-done.1.got_a = f32[280,128]{1,0:T(8,128)S(1)} collective-permute-done((f32[280,128]{1,0:T(8,128)}, f32[280,128]{1,0:T(8,128)S(1)}, u32[]{:S(2)}, u32[]{:S(2)}) %collective-permute-start.1) | collective-permute-done | bytes 143392 | tf_op jit(solution)/shard_map/ppermute | solution.py:348
  10.1 0.3 collective-permute-start.3
  10.4 0.1 pad_add_fusion.place
  10.5 0.0 copy-done.2
  10.5 0.7 %copy-done.3 = s32[512]{0:T(512)S(1)} copy-done((s32[512]{0:T(512)S(1)}, s32[512]{0:T(512)}, u32[]{:S(2)}) %copy-start.3) | copy-done | bytes 2072
  11.2 0.9 %copy-done = f32[280,128]{1,0:T(8,128)S(1)} copy-done((f32[280,128]{1,0:T(8,128)S(1)}, f32[280,128]{1,0:T(8,128)}, u32[]{:S(2)}) %copy-start) | copy-done | bytes 143384
  12.1 1.5 %own.1 = (f32[4,128,128]{2,1,0:T(8,128)S(1)}, bf16[256,256]{1,0:T(8,128)(2,1)S(1)}, bf16[512,512]{1,0:T(8,128)(2,1)S(1)}, bf16[512,128]{1,0:T(8,128)(2,1)S(1)}) custom-call(s32[2]{0:T(128)S(1)} %pad_add_fusion.place, f32[280,128]{1,0:T(8,128)S(1)} %copy-done, f32[8,256]{1,0:T(8,128)S(1)} %copy-done.2, s32[1,512]{1,0:T(1,128)S(1)} %bitcast.8), custom_call_target="tpu_custom_call" | custom-call | flops 1000000000 | bytes 1000000 | tf_op jit(solution)/shard_map/own/pallas_call | solution.py:385
  13.6 0.0 copy-start.1
  13.6 0.0 collective-permute-done.2.got_b
  13.6 1.8 %collective-permute-start.4 = (f32[280,128]{1,0:T(8,128)S(1)}, f32[280,128]{1,0:T(8,128)S(1)}, u32[]{:S(2)}, u32[]{:S(2)}) collective-permute-start(f32[280,128]{1,0:T(8,128)S(1)} %collective-permute-done.2.got_b), channel_id=1, source_target_pairs={{0,4},{4,0},{8,12},{12,8},{16,20},{20,16},{24,28},{28,24},{32,36},... | collective-permute-start | bytes 430088 | tf_op jit(solution)/shard_map/ppermute | solution.py:348
  15.5 0.0 collective-permute-done.inner
  15.5 0.3 collective-permute-done.3.relay_a
  15.7 2.4 %near.1.near_cells = f32[12,128,128]{2,1,0:T(8,128)S(1)} custom-call(s32[2]{0:T(128)S(1)} %pad_add_fusion.place, f32[280,128]{1,0:T(8,128)S(1)} %collective-permute-done.inner, f32[280,128]{1,0:T(8,128)S(1)} %collective-permute-done.1.got_a, f32[280,128]{1,0:T(8,128)S(1)} %collective-permute-done.2.got_b, f32[280,128]{1,0:T(8,128)S(1)} %collective-permute-done.3.relay_a), custom_call_target="tpu_custom_call" | custom-call | flops 2000000000 | bytes 1000000 | tf_op jit(solution)/shard_map/near/pallas_call | solution.py:400
  18.1 0.7 %collective-permute-done.4.relay_b = f32[280,128]{1,0:T(8,128)S(1)} collective-permute-done((f32[280,128]{1,0:T(8,128)S(1)}, f32[280,128]{1,0:T(8,128)S(1)}, u32[]{:S(2)}, u32[]{:S(2)}) %collective-permute-start.4) | collective-permute-done | bytes 143392 | tf_op jit(solution)/shard_map/ppermute | solution.py:348
  18.8 4.0 %filter.1.own = f32[256,128]{1,0:T(8,128)S(1)} custom-call(s32[2]{0:T(128)S(1)} %pad_add_fusion.place, f32[280,128]{1,0:T(8,128)S(1)} %copy-done.1, f32[280,128]{1,0:T(8,128)S(1)} %collective-permute-done.inner, f32[280,128]{1,0:T(8,128)S(1)} %collective-permute-done.1.got_a, f32[280,128]{1,0:T(8,128)S(1)} %collective-permute-done.2.got_b, ...), custom_call_target="tpu_custom_call" | custom-call | tf_op jit(solution)/shard_map/filter/pallas_call | solution.py:411
  22.9 7.3 %all_gather.3.states = f32[256,512]{1,0:T(8,128)S(1)} all-gather(f32[256,128]{1,0:T(8,128)S(1)} %filter.1.own), channel_id=1, replica_groups=mesh['dom'=64,'band'=4] {'band'}, dimensions={1}, use_global_device_ids=true | all-gather | bytes 655360 | tf_op jit(solution)/shard_map/all_gather | solution.py:429
  30.2 1.4 %margin.1 = (f32[512,128]{1,0:T(8,128)S(1)}, f32[256,128]{1,0:T(8,128)}) custom-call(f32[256,512]{1,0:T(8,128)S(1)} %all_gather.3.states, bf16[512,512]{1,0:T(8,128)(2,1)S(1)} %get-tuple-element.13.pick, bf16[512,128]{1,0:T(8,128)(2,1)S(1)} %get-tuple-element.14.own_pick, f32[256,128]{1,0:T(8,128)S(1)} %filter.1.own, bf16[256,256]{1,0:T(8,128)(2,1)S(1)} %get-tuple-element.15.back), custom_call_target="tpu_custom_call" | custom-call | tf_op jit(solution)/shard_map/margin/pallas_call | solution.py:430
  31.6 33.3 %all_to_all.5 = f32[64,8,128]{2,1,0:T(8,128)S(1)} all-to-all(f32[64,8,128]{2,1,0:T(8,128)S(1)} %bitcast.7), channel_id=1, replica_groups=mesh['dom'=64,'band'=4] {'dom'}, dimensions={0} | all-to-all | bytes 524288 | tf_op jit(solution)/shard_map/all_to_all | solution.py:440
  64.9 0.1 reduce_sum.9
  65.0 0.6 broadcast_multiply_fusion
  (4 shorter events, 0.0 us)
Async XLA Ops:
  3.1 7.1 %collective-permute-start.1 = (f32[280,128]{1,0:T(8,128)}, f32[280,128]{1,0:T(8,128)S(1)}, u32[]{:S(2)}, u32[]{:S(2)}) collective-permute-start(f32[280,128]{1,0:T(8,128)} %get-tuple-element.10.packed), channel_id=1, source_target_pairs={{0,12},{12,0},{4,8},{8,4},{16,28},{28,16},{20,24},{24,20},{32,44},... | collective-permute-start | bytes 430088 | tf_op jit(solution)/shard_map/ppermute | solution.py:348
  6.2 7.5 %collective-permute-start.2 = (f32[280,128]{1,0:T(8,128)}, f32[280,128]{1,0:T(8,128)S(1)}, u32[]{:S(2)}, u32[]{:S(2)}) collective-permute-start(f32[280,128]{1,0:T(8,128)} %get-tuple-element.10.packed), channel_id=1, source_target_pairs={{8,20},{20,8},{12,16},{16,12},{24,36},{36,24},{28,32},{32,28},{40,... | collective-permute-start | bytes 430088 | tf_op jit(solution)/shard_map/ppermute | solution.py:348
  6.8 8.6 %collective-permute-start = (f32[280,128]{1,0:T(8,128)}, f32[280,128]{1,0:T(8,128)S(1)}, u32[]{:S(2)}, u32[]{:S(2)}) collective-permute-start(f32[280,128]{1,0:T(8,128)} %get-tuple-element.10.packed), channel_id=1, source_target_pairs={{0,4},{4,0},{8,12},{12,8},{16,20},{20,16},{24,28},{28,24},{32,36},... | collective-permute-start | bytes 430088 | tf_op jit(solution)/shard_map/ppermute | solution.py:348
  7.1 3.5 %copy-start.2 = (f32[8,256]{1,0:T(8,128)S(1)}, f32[8,256]{1,0:T(8,128)}, u32[]{:S(2)}) copy-start(f32[8,256]{1,0:T(8,128)} %get-tuple-element.11.rank) | copy-start | bytes 24580
  10.1 5.6 %collective-permute-start.3 = (f32[280,128]{1,0:T(8,128)S(1)}, f32[280,128]{1,0:T(8,128)S(1)}, u32[]{:S(2)}, u32[]{:S(2)}) collective-permute-start(f32[280,128]{1,0:T(8,128)S(1)} %collective-permute-done.1.got_a), channel_id=1, source_target_pairs={{0,4},{4,0},{8,12},{12,8},{16,20},{20,16},{24,28},{28,24},{32,36},... | collective-permute-start | bytes 430088 | tf_op jit(solution)/shard_map/ppermute | solution.py:348
  10.5 0.7 %copy-start.3 = (s32[512]{0:T(512)S(1)}, s32[512]{0:T(512)}, u32[]{:S(2)}) copy-start(s32[512]{0:T(512)} %param.11) | copy-start | bytes 6148
  11.2 0.9 %copy-start = (f32[280,128]{1,0:T(8,128)S(1)}, f32[280,128]{1,0:T(8,128)}, u32[]{:S(2)}) copy-start(f32[280,128]{1,0:T(8,128)} %get-tuple-element.10.packed) | copy-start | bytes 430084
  13.6 5.2 %copy-start.1 = (f32[280,128]{1,0:T(8,128)S(1)}, f32[280,128]{1,0:T(8,128)}, u32[]{:S(2)}) copy-start(f32[280,128]{1,0:T(8,128)} %get-tuple-element.10.packed) | copy-start | bytes 430084
  13.6 5.2 %collective-permute-start.4 = (f32[280,128]{1,0:T(8,128)S(1)}, f32[280,128]{1,0:T(8,128)S(1)}, u32[]{:S(2)}, u32[]{:S(2)}) collective-permute-start(f32[280,128]{1,0:T(8,128)S(1)} %collective-permute-done.2.got_b), channel_id=1, source_target_pairs={{0,4},{4,0},{8,12},{12,8},{16,20},{20,16},{24,28},{28,24},{32,36},... | collective-permute-start | bytes 430088 | tf_op jit(solution)/shard_map/ppermute | solution.py:348

commit v5 on v4

--- a/solution.py
+++ b/solution.py
@@ -27,6 +27,14 @@
 ANY = pl.BlockSpec(memory_space=pl.ANY)
 f32 = jnp.float32
 bf16 = jnp.bfloat16
+
+
+def final_gain():
+    sigma = gain = sigma_first
+    for _ in range(DEGREE - 1):
+        sigma = 1.0 / (gamma_value - sigma)
+        gain = gain * 2.0 * sigma
+    return gain
 
 
 def dot(a, b):
@@ -96,6 +104,10 @@
     corner_id = corners.astype(f32)
     plane_count = plane.shape[1]
     plane_row = jnp.concatenate([plane_in[...].astype(f32), jnp.full((1, 128 - plane_count), -1.0, f32)], 1)
+
+    scale = lax.rsqrt(rows_in[1:2, :])
+    copies[0].wait()
+    field_terms = jnp.concatenate(exact(field_in[...] * column_of(scale)), 1)
 
     row_id = iota((nodes, nodes), 0).astype(f32)
     lane_id = iota((nodes, nodes), 1).astype(f32)
@@ -151,17 +163,14 @@
         out[at + 1 : at + 2, :] = jnp.where(low_lane, chance_turned, chance)[0:1]
 
     move = flag(row_id == rank)
-    scale = lax.rsqrt(rows_in[1:2, :])
     terms = jnp.concatenate([t.astype(f32) for t in exact(scale)] + [jnp.zeros((13, nodes), f32)], 0)
     moved = dot_t(terms.astype(bf16), move)
     scale = moved[0:1] + moved[1:2] + moved[2:3]
     out[nodes + 20 : nodes + 21, :] = scale[:, :128]
     out[nodes + 21 : nodes + 22, :] = scale[:, 128:]
     out[nodes + 22 : nodes + 24, :] = jnp.zeros((2, 128), f32)
-    copies[0].wait()
-    sorted_field = dot(move, jnp.concatenate(exact(field_in[...]), 1))
-    sorted_field = sorted_field[:, :width] + sorted_field[:, width : 2 * width] + sorted_field[:, 2 * width :]
-    out[:nodes, :] = sorted_field * column_of(scale)
+    sorted_field = dot(move, field_terms)
+    out[:nodes, :] = sorted_field[:, :width] + sorted_field[:, width : 2 * width] + sorted_field[:, 2 * width :]
 
 
 def layer_matrix(table, layer, scratch):
@@ -300,20 +309,14 @@
     for q, value in enumerate(window(field_part)):
         field_a[nodes * q : nodes * (q + 1), :] = value
         put(even, nodes * q, value)
-    sigma_last = sigma_first
     final = []
     for k in range(1, DEGREE + 1):
         source, target = (even, odd) if k % 2 else (odd, even)
         newer = field_b if k % 2 else field_a
-        if k == 1:
-            gain, keep = sigma_first, None
-        else:
-            sigma_next = 1.0 / (gamma_value - sigma_last)
-            gain, keep = 2.0 * sigma_next, sigma_last * sigma_next
-            sigma_last = sigma_next
+        keep = {1: None, 2: 0.5}.get(k, 0.25)
         for j in range(k // 2, pairs - k // 2):
             product = dot(bands[j], source[128 * j : 128 * j + 256, :])
-            value = gain * (product[:128, :width] + (product[:128, width:] + product[128:, :width]))
+            value = product[:128, :width] + (product[:128, width:] + product[128:, :width])
             if keep is not None:
                 value = value - keep * newer[128 * j : 128 * (j + 1), :]
             if k == DEGREE:
@@ -321,8 +324,8 @@
             else:
                 newer[128 * j : 128 * (j + 1), :] = value
                 put(target, 128 * j, value)
-    scale = column_of(jnp.concatenate([tables[REACH][20:21], tables[REACH][21:22]], 1))
-    out[...] = jnp.concatenate(final, 0) / scale
+    out[...] = jnp.concatenate(final, 0) * (final_gain() / column_of(
+        jnp.concatenate([tables[REACH][20:21], tables[REACH][21:22]], 1)))
 
 
 def margin_kernel(states, pick, own_pick, own, back, out, filtered, original, sem):

time: 65.8 us -> 65.7 us (level)
  no operation moved by 1% of the time
where the time goes in v5:
time: 65.7 us; the launch traced here: 65.5 us
  blocking collectives  40.6 us (62%)
  Pallas kernels  11.7 us (18%)
  starting transfers between devices  6.1 us (9%)
  waiting for transfers between devices  4.07 us (6%)
  local copies, waits for them, and re-layouts  1.59 us (2%)
  other arithmetic  0.74 us (1%)
  between operations  0.7 us (1%)
    all_to_all x1, blocking collectives, shards(): lax.all_to_all(term.reshape(doms, rows, width), 'dom', 0, 0, tiled=True)  33.3 us
    all_gather x1, blocking collectives, shards(): all_states = lax.all_gather(by_layer, 'band', axis=1, tiled=True)  7.34 us
    ppermute x5, starting transfers between devices, swapped(): return lax.ppermute(block, axis, route)  6.1 us
    ppermute x5, waiting for transfers between devices, swapped(): return lax.ppermute(block, axis, route)  4.07 us
    pallas_call x1, Pallas kernels, shards(): pl.pallas_call(filter_kernel, out_shape=jax.ShapeDtypeStruct((nodes, widt...  3.98 us
    pallas_call x1, Pallas kernels, shards(): pl.pallas_call(near_kernel, out_shape=jax.ShapeDtypeStruct((3 * LAYERS, 1...  2.37 us
    pallas_call x1, Pallas kernels, shards(): pl.pallas_call(sort_kernel, out_shape=[jax.ShapeDtypeStruct((nodes + EXTR...  2.35 us
    unnamed x8, local copies, waits for them, and re-layouts  1.59 us
  transfers between devices with their start and end apart: 5, of which 3 were waited for; matrix products, arithmetic and copies ran while one was open for 0% of the time, Pallas kernels for 6%

profile of v5, /device:TPU:32, one launch (start us, length us, event | category | flops | bytes accessed | tf_op | source)
XLA Modules:
  0.0 65.5 jit_solution(9508306366018441448)
XLA Ops:
  0.6 2.3 %sort.1 = (f32[280,128]{1,0:T(8,128)}, f32[8,256]{1,0:T(8,128)}) custom-call(f32[256,128]{1,0:T(8,128)} %field.1, s32[8,256]{1,0:T(8,128)} %links.1, f32[1,256]{1,0:T(1,128)} %bitcast.9, f32[1,256]{1,0:T(1,128)} %bitcast.10, s32[1,64]{1,0:T(1,128)} %bitcast.11), custom_call_target="tpu_custom_call" | custom-call | tf_op jit(solution)/shard_map/sort/pallas_call | solution.py:365
  3.0 3.1 %collective-permute-start.1 = (f32[280,128]{1,0:T(8,128)}, f32[280,128]{1,0:T(8,128)S(1)}, u32[]{:S(2)}, u32[]{:S(2)}) collective-permute-start(f32[280,128]{1,0:T(8,128)} %get-tuple-element.10.packed), channel_id=1, source_target_pairs={{0,12},{12,0},{4,8},{8,4},{16,28},{28,16},{20,24},{24,20},{32,44},... | collective-permute-start | bytes 430088 | tf_op jit(solution)/shard_map/ppermute | solution.py:351
  6.1 0.7 %collective-permute-start.2 = (f32[280,128]{1,0:T(8,128)}, f32[280,128]{1,0:T(8,128)S(1)}, u32[]{:S(2)}, u32[]{:S(2)}) collective-permute-start(f32[280,128]{1,0:T(8,128)} %get-tuple-element.10.packed), channel_id=1, source_target_pairs={{8,20},{20,8},{12,16},{16,12},{24,36},{36,24},{28,32},{32,28},{40,... | collective-permute-start | bytes 430088 | tf_op jit(solution)/shard_map/ppermute | solution.py:351
  6.7 0.2 collective-permute-start
  7.0 3.1 %collective-permute-done.1.got_a = f32[280,128]{1,0:T(8,128)S(1)} collective-permute-done((f32[280,128]{1,0:T(8,128)}, f32[280,128]{1,0:T(8,128)S(1)}, u32[]{:S(2)}, u32[]{:S(2)}) %collective-permute-start.1) | collective-permute-done | bytes 143392 | tf_op jit(solution)/shard_map/ppermute | solution.py:351
  10.1 0.3 collective-permute-start.3
  10.4 0.1 pad_add_fusion.place
  10.4 0.0 copy-done.2
  10.4 0.7 %copy-done.3 = s32[512]{0:T(512)S(1)} copy-done((s32[512]{0:T(512)S(1)}, s32[512]{0:T(512)}, u32[]{:S(2)}) %copy-start.3) | copy-done | bytes 2072
  11.1 0.9 %copy-done = f32[280,128]{1,0:T(8,128)S(1)} copy-done((f32[280,128]{1,0:T(8,128)S(1)}, f32[280,128]{1,0:T(8,128)}, u32[]{:S(2)}) %copy-start) | copy-done | bytes 143384
  12.0 1.5 %own.1 = (f32[4,128,128]{2,1,0:T(8,128)S(1)}, bf16[256,256]{1,0:T(8,128)(2,1)S(1)}, bf16[512,512]{1,0:T(8,128)(2,1)S(1)}, bf16[512,128]{1,0:T(8,128)(2,1)S(1)}) custom-call(s32[2]{0:T(128)S(1)} %pad_add_fusion.place, f32[280,128]{1,0:T(8,128)S(1)} %copy-done, f32[8,256]{1,0:T(8,128)S(1)} %copy-done.2, s32[1,512]{1,0:T(1,128)S(1)} %bitcast.8), custom_call_target="tpu_custom_call" | custom-call | flops 1000000000 | bytes 1000000 | tf_op jit(solution)/shard_map/own/pallas_call | solution.py:388
  13.6 0.0 copy-start.1
  13.6 0.0 collective-permute-done.2.got_b
  13.6 1.8 %collective-permute-start.4 = (f32[280,128]{1,0:T(8,128)S(1)}, f32[280,128]{1,0:T(8,128)S(1)}, u32[]{:S(2)}, u32[]{:S(2)}) collective-permute-start(f32[280,128]{1,0:T(8,128)S(1)} %collective-permute-done.2.got_b), channel_id=1, source_target_pairs={{0,4},{4,0},{8,12},{12,8},{16,20},{20,16},{24,28},{28,24},{32,36},... | collective-permute-start | bytes 430088 | tf_op jit(solution)/shard_map/ppermute | solution.py:351
  15.4 0.0 collective-permute-done.inner
  15.4 0.2 collective-permute-done.3.relay_a
  15.6 2.4 %near.1.near_cells = f32[12,128,128]{2,1,0:T(8,128)S(1)} custom-call(s32[2]{0:T(128)S(1)} %pad_add_fusion.place, f32[280,128]{1,0:T(8,128)S(1)} %collective-permute-done.inner, f32[280,128]{1,0:T(8,128)S(1)} %collective-permute-done.1.got_a, f32[280,128]{1,0:T(8,128)S(1)} %collective-permute-done.2.got_b, f32[280,128]{1,0:T(8,128)S(1)} %collective-permute-done.3.relay_a), custom_call_target="tpu_custom_call" | custom-call | flops 2000000000 | bytes 1000000 | tf_op jit(solution)/shard_map/near/pallas_call | solution.py:403
  18.0 0.7 %collective-permute-done.4.relay_b = f32[280,128]{1,0:T(8,128)S(1)} collective-permute-done((f32[280,128]{1,0:T(8,128)S(1)}, f32[280,128]{1,0:T(8,128)S(1)}, u32[]{:S(2)}, u32[]{:S(2)}) %collective-permute-start.4) | collective-permute-done | bytes 143392 | tf_op jit(solution)/shard_map/ppermute | solution.py:351
  18.8 4.0 %filter.1.own = f32[256,128]{1,0:T(8,128)S(1)} custom-call(s32[2]{0:T(128)S(1)} %pad_add_fusion.place, f32[280,128]{1,0:T(8,128)S(1)} %copy-done.1, f32[280,128]{1,0:T(8,128)S(1)} %collective-permute-done.inner, f32[280,128]{1,0:T(8,128)S(1)} %collective-permute-done.1.got_a, f32[280,128]{1,0:T(8,128)S(1)} %collective-permute-done.2.got_b, ...), custom_call_target="tpu_custom_call" | custom-call | tf_op jit(solution)/shard_map/filter/pallas_call | solution.py:414
  22.7 7.3 %all_gather.3.states = f32[256,512]{1,0:T(8,128)S(1)} all-gather(f32[256,128]{1,0:T(8,128)S(1)} %filter.1.own), channel_id=1, replica_groups=mesh['dom'=64,'band'=4] {'band'}, dimensions={1}, use_global_device_ids=true | all-gather | bytes 655360 | tf_op jit(solution)/shard_map/all_gather | solution.py:432
  30.1 1.4 %margin.1 = (f32[512,128]{1,0:T(8,128)S(1)}, f32[256,128]{1,0:T(8,128)}) custom-call(f32[256,512]{1,0:T(8,128)S(1)} %all_gather.3.states, bf16[512,512]{1,0:T(8,128)(2,1)S(1)} %get-tuple-element.13.pick, bf16[512,128]{1,0:T(8,128)(2,1)S(1)} %get-tuple-element.14.own_pick, f32[256,128]{1,0:T(8,128)S(1)} %filter.1.own, bf16[256,256]{1,0:T(8,128)(2,1)S(1)} %get-tuple-element.15.back), custom_call_target="tpu_custom_call" | custom-call | tf_op jit(solution)/shard_map/margin/pallas_call | solution.py:433
  31.5 33.3 %all_to_all.5 = f32[64,8,128]{2,1,0:T(8,128)S(1)} all-to-all(f32[64,8,128]{2,1,0:T(8,128)S(1)} %bitcast.7), channel_id=1, replica_groups=mesh['dom'=64,'band'=4] {'dom'}, dimensions={0} | all-to-all | bytes 524288 | tf_op jit(solution)/shard_map/all_to_all | solution.py:443
  64.8 0.1 reduce_sum.9
  64.9 0.6 broadcast_multiply_fusion
  (4 shorter events, 0.0 us)
Async XLA Ops:
  3.0 7.1 %collective-permute-start.1 = (f32[280,128]{1,0:T(8,128)}, f32[280,128]{1,0:T(8,128)S(1)}, u32[]{:S(2)}, u32[]{:S(2)}) collective-permute-start(f32[280,128]{1,0:T(8,128)} %get-tuple-element.10.packed), channel_id=1, source_target_pairs={{0,12},{12,0},{4,8},{8,4},{16,28},{28,16},{20,24},{24,20},{32,44},... | collective-permute-start | bytes 430088 | tf_op jit(solution)/shard_map/ppermute | solution.py:351
  6.1 7.5 %collective-permute-start.2 = (f32[280,128]{1,0:T(8,128)}, f32[280,128]{1,0:T(8,128)S(1)}, u32[]{:S(2)}, u32[]{:S(2)}) collective-permute-start(f32[280,128]{1,0:T(8,128)} %get-tuple-element.10.packed), channel_id=1, source_target_pairs={{8,20},{20,8},{12,16},{16,12},{24,36},{36,24},{28,32},{32,28},{40,... | collective-permute-start | bytes 430088 | tf_op jit(solution)/shard_map/ppermute | solution.py:351
  6.7 8.6 %collective-permute-start = (f32[280,128]{1,0:T(8,128)}, f32[280,128]{1,0:T(8,128)S(1)}, u32[]{:S(2)}, u32[]{:S(2)}) collective-permute-start(f32[280,128]{1,0:T(8,128)} %get-tuple-element.10.packed), channel_id=1, source_target_pairs={{0,4},{4,0},{8,12},{12,8},{16,20},{20,16},{24,28},{28,24},{32,36},... | collective-permute-start | bytes 430088 | tf_op jit(solution)/shard_map/ppermute | solution.py:351
  7.0 3.5 %copy-start.2 = (f32[8,256]{1,0:T(8,128)S(1)}, f32[8,256]{1,0:T(8,128)}, u32[]{:S(2)}) copy-start(f32[8,256]{1,0:T(8,128)} %get-tuple-element.11.rank) | copy-start | bytes 24580
  10.1 5.6 %collective-permute-start.3 = (f32[280,128]{1,0:T(8,128)S(1)}, f32[280,128]{1,0:T(8,128)S(1)}, u32[]{:S(2)}, u32[]{:S(2)}) collective-permute-start(f32[280,128]{1,0:T(8,128)S(1)} %collective-permute-done.1.got_a), channel_id=1, source_target_pairs={{0,4},{4,0},{8,12},{12,8},{16,20},{20,16},{24,28},{28,24},{32,36},... | collective-permute-start | bytes 430088 | tf_op jit(solution)/shard_map/ppermute | solution.py:351
  10.4 0.7 %copy-start.3 = (s32[512]{0:T(512)S(1)}, s32[512]{0:T(512)}, u32[]{:S(2)}) copy-start(s32[512]{0:T(512)} %param.11) | copy-start | bytes 6148
  11.1 0.9 %copy-start = (f32[280,128]{1,0:T(8,128)S(1)}, f32[280,128]{1,0:T(8,128)}, u32[]{:S(2)}) copy-start(f32[280,128]{1,0:T(8,128)} %get-tuple-element.10.packed) | copy-start | bytes 430084
  13.6 5.2 %copy-start.1 = (f32[280,128]{1,0:T(8,128)S(1)}, f32[280,128]{1,0:T(8,128)}, u32[]{:S(2)}) copy-start(f32[280,128]{1,0:T(8,128)} %get-tuple-element.10.packed) | copy-start | bytes 430084
  13.6 5.2 %collective-permute-start.4 = (f32[280,128]{1,0:T(8,128)S(1)}, f32[280,128]{1,0:T(8,128)S(1)}, u32[]{:S(2)}, u32[]{:S(2)}) collective-permute-start(f32[280,128]{1,0:T(8,128)S(1)} %collective-permute-done.2.got_b), channel_id=1, source_target_pairs={{0,4},{4,0},{8,12},{12,8},{16,20},{20,16},{24,28},{28,24},{32,36},... | collective-permute-start | bytes 430088 | tf_op jit(solution)/shard_map/ppermute | solution.py:351

commit v6 on v5

--- a/solution.py
+++ b/solution.py
@@ -1,3 +1,5 @@
+import functools
+
 import jax
 import jax.numpy as jnp
 import numpy as np
@@ -328,7 +330,7 @@
         jnp.concatenate([tables[REACH][20:21], tables[REACH][21:22]], 1)))
 
 
-def margin_kernel(states, pick, own_pick, own, back, out, filtered, original, sem):
+def margin_kernel(total_nodes, states, pick, own_pick, own, back, out, filtered, original, sem):
     width = out.shape[1]
     moved = dot(back[...], jnp.concatenate(exact(own[...]), 1))
     original[...] = moved[:, :width] + moved[:, width : 2 * width] + moved[:, 2 * width :]
@@ -339,7 +341,7 @@
     own_low = dot(low, own_pick[...]).astype(bf16)
     part = cross(own_high, high) + cross(own_high, low) + cross(own_low, high)
     chosen = [dot(term, pick[...]) for term in exact(part)]
-    out[...] = (chosen[0] + chosen[1] + chosen[2]).T
+    out[...] = ((chosen[0] + chosen[1] + chosen[2]) * (1.0 / total_nodes)).T
     copy.wait()
 
 
@@ -431,7 +433,7 @@
 
     all_states = lax.all_gather(by_layer, "band", axis=1, tiled=True)
     term, filtered = pl.pallas_call(
-        margin_kernel,
+        functools.partial(margin_kernel, nodes * doms),
         out_shape=[jax.ShapeDtypeStruct((states, width), f32), jax.ShapeDtypeStruct((nodes, width), f32)],
         in_specs=[VMEM] * 5,
         out_specs=[VMEM, ANY],
@@ -441,7 +443,7 @@
     )(all_states, pick, own_pick, by_layer, back)
     rows = state_order.shape[0] // doms
     parts = lax.all_to_all(term.reshape(doms, rows, width), "dom", 0, 0, tiled=True)
-    return (filtered, parts.sum(0) * (1.0 / (nodes * doms)))
+    return (filtered, parts.sum(0))
 
 
 def solution(mesh):

time: 65.7 us -> 65.7 us (level)
  no operation moved by 1% of the time
where the time goes in v6:
time: 65.7 us; the launch traced here: 65.5 us
  blocking collectives  40.6 us (62%)
  Pallas kernels  11.7 us (18%)
  starting transfers between devices  6.1 us (9%)
  waiting for transfers between devices  4.07 us (6%)
  local copies, waits for them, and re-layouts  1.59 us (2%)
  other arithmetic  0.73 us (1%)
  between operations  0.7 us (1%)
    all_to_all x1, blocking collectives, shards(): lax.all_to_all(term.reshape(doms, rows, width), 'dom', 0, 0, tiled=True)  33.3 us
    all_gather x1, blocking collectives, shards(): all_states = lax.all_gather(by_layer, 'band', axis=1, tiled=True)  7.34 us
    ppermute x5, starting transfers between devices, swapped(): return lax.ppermute(block, axis, route)  6.1 us
    ppermute x5, waiting for transfers between devices, swapped(): return lax.ppermute(block, axis, route)  4.07 us
    pallas_call x1, Pallas kernels, shards(): pl.pallas_call(filter_kernel, out_shape=jax.ShapeDtypeStruct((nodes, widt...  3.98 us
    pallas_call x1, Pallas kernels, shards(): pl.pallas_call(near_kernel, out_shape=jax.ShapeDtypeStruct((3 * LAYERS, 1...  2.37 us
    pallas_call x1, Pallas kernels, shards(): pl.pallas_call(sort_kernel, out_shape=[jax.ShapeDtypeStruct((nodes + EXTR...  2.35 us
    unnamed x8, local copies, waits for them, and re-layouts  1.59 us
  transfers between devices with their start and end apart: 5, of which 3 were waited for; matrix products, arithmetic and copies ran while one was open for 0% of the time, Pallas kernels for 6%

profile of v6, /device:TPU:32, one launch (start us, length us, event | category | flops | bytes accessed | tf_op | source)
XLA Modules:
  0.0 65.5 jit_solution(12035911031275674220)
XLA Ops:
  0.6 2.3 %sort.1 = (f32[280,128]{1,0:T(8,128)}, f32[8,256]{1,0:T(8,128)}) custom-call(f32[256,128]{1,0:T(8,128)} %field.1, s32[8,256]{1,0:T(8,128)} %links.1, f32[1,256]{1,0:T(1,128)} %bitcast.9, f32[1,256]{1,0:T(1,128)} %bitcast.10, s32[1,64]{1,0:T(1,128)} %bitcast.11), custom_call_target="tpu_custom_call" | custom-call | tf_op jit(solution)/shard_map/sort/pallas_call | solution.py:367
  3.0 3.1 %collective-permute-start.1 = (f32[280,128]{1,0:T(8,128)}, f32[280,128]{1,0:T(8,128)S(1)}, u32[]{:S(2)}, u32[]{:S(2)}) collective-permute-start(f32[280,128]{1,0:T(8,128)} %get-tuple-element.10.packed), channel_id=1, source_target_pairs={{0,12},{12,0},{4,8},{8,4},{16,28},{28,16},{20,24},{24,20},{32,44},... | collective-permute-start | bytes 430088 | tf_op jit(solution)/shard_map/ppermute | solution.py:353
  6.1 0.7 %collective-permute-start.2 = (f32[280,128]{1,0:T(8,128)}, f32[280,128]{1,0:T(8,128)S(1)}, u32[]{:S(2)}, u32[]{:S(2)}) collective-permute-start(f32[280,128]{1,0:T(8,128)} %get-tuple-element.10.packed), channel_id=1, source_target_pairs={{8,20},{20,8},{12,16},{16,12},{24,36},{36,24},{28,32},{32,28},{40,... | collective-permute-start | bytes 430088 | tf_op jit(solution)/shard_map/ppermute | solution.py:353
  6.7 0.2 collective-permute-start
  7.0 3.1 %collective-permute-done.1.got_a = f32[280,128]{1,0:T(8,128)S(1)} collective-permute-done((f32[280,128]{1,0:T(8,128)}, f32[280,128]{1,0:T(8,128)S(1)}, u32[]{:S(2)}, u32[]{:S(2)}) %collective-permute-start.1) | collective-permute-done | bytes 143392 | tf_op jit(solution)/shard_map/ppermute | solution.py:353
  10.1 0.3 collective-permute-start.3
  10.4 0.1 pad_add_fusion.place
  10.4 0.0 copy-done.2
  10.4 0.7 %copy-done.3 = s32[512]{0:T(512)S(1)} copy-done((s32[512]{0:T(512)S(1)}, s32[512]{0:T(512)}, u32[]{:S(2)}) %copy-start.3) | copy-done | bytes 2072
  11.1 0.9 %copy-done = f32[280,128]{1,0:T(8,128)S(1)} copy-done((f32[280,128]{1,0:T(8,128)S(1)}, f32[280,128]{1,0:T(8,128)}, u32[]{:S(2)}) %copy-start) | copy-done | bytes 143384
  12.0 1.5 %own.1 = (f32[4,128,128]{2,1,0:T(8,128)S(1)}, bf16[256,256]{1,0:T(8,128)(2,1)S(1)}, bf16[512,512]{1,0:T(8,128)(2,1)S(1)}, bf16[512,128]{1,0:T(8,128)(2,1)S(1)}) custom-call(s32[2]{0:T(128)S(1)} %pad_add_fusion.place, f32[280,128]{1,0:T(8,128)S(1)} %copy-done, f32[8,256]{1,0:T(8,128)S(1)} %copy-done.2, s32[1,512]{1,0:T(1,128)S(1)} %bitcast.8), custom_call_target="tpu_custom_call" | custom-call | flops 1000000000 | bytes 1000000 | tf_op jit(solution)/shard_map/own/pallas_call | solution.py:390
  13.6 0.0 copy-start.1
  13.6 0.0 collective-permute-done.2.got_b
  13.6 1.8 %collective-permute-start.4 = (f32[280,128]{1,0:T(8,128)S(1)}, f32[280,128]{1,0:T(8,128)S(1)}, u32[]{:S(2)}, u32[]{:S(2)}) collective-permute-start(f32[280,128]{1,0:T(8,128)S(1)} %collective-permute-done.2.got_b), channel_id=1, source_target_pairs={{0,4},{4,0},{8,12},{12,8},{16,20},{20,16},{24,28},{28,24},{32,36},... | collective-permute-start | bytes 430088 | tf_op jit(solution)/shard_map/ppermute | solution.py:353
  15.4 0.0 collective-permute-done.inner
  15.4 0.2 collective-permute-done.3.relay_a
  15.6 2.4 %near.1.near_cells = f32[12,128,128]{2,1,0:T(8,128)S(1)} custom-call(s32[2]{0:T(128)S(1)} %pad_add_fusion.place, f32[280,128]{1,0:T(8,128)S(1)} %collective-permute-done.inner, f32[280,128]{1,0:T(8,128)S(1)} %collective-permute-done.1.got_a, f32[280,128]{1,0:T(8,128)S(1)} %collective-permute-done.2.got_b, f32[280,128]{1,0:T(8,128)S(1)} %collective-permute-done.3.relay_a), custom_call_target="tpu_custom_call" | custom-call | flops 2000000000 | bytes 1000000 | tf_op jit(solution)/shard_map/near/pallas_call | solution.py:405
  18.0 0.7 %collective-permute-done.4.relay_b = f32[280,128]{1,0:T(8,128)S(1)} collective-permute-done((f32[280,128]{1,0:T(8,128)S(1)}, f32[280,128]{1,0:T(8,128)S(1)}, u32[]{:S(2)}, u32[]{:S(2)}) %collective-permute-start.4) | collective-permute-done | bytes 143392 | tf_op jit(solution)/shard_map/ppermute | solution.py:353
  18.8 0.0 copy-done.1
  18.8 4.0 %filter.1.own = f32[256,128]{1,0:T(8,128)S(1)} custom-call(s32[2]{0:T(128)S(1)} %pad_add_fusion.place, f32[280,128]{1,0:T(8,128)S(1)} %copy-done.1, f32[280,128]{1,0:T(8,128)S(1)} %collective-permute-done.inner, f32[280,128]{1,0:T(8,128)S(1)} %collective-permute-done.1.got_a, f32[280,128]{1,0:T(8,128)S(1)} %collective-permute-done.2.got_b, ...), custom_call_target="tpu_custom_call" | custom-call | tf_op jit(solution)/shard_map/filter/pallas_call | solution.py:416
  22.7 7.3 %all_gather.3.states = f32[256,512]{1,0:T(8,128)S(1)} all-gather(f32[256,128]{1,0:T(8,128)S(1)} %filter.1.own), channel_id=1, replica_groups=mesh['dom'=64,'band'=4] {'band'}, dimensions={1}, use_global_device_ids=true | all-gather | bytes 655360 | tf_op jit(solution)/shard_map/all_gather | solution.py:434
  30.1 1.4 %margin.1 = (f32[512,128]{1,0:T(8,128)S(1)}, f32[256,128]{1,0:T(8,128)}) custom-call(f32[256,512]{1,0:T(8,128)S(1)} %all_gather.3.states, bf16[512,512]{1,0:T(8,128)(2,1)S(1)} %get-tuple-element.13.pick, bf16[512,128]{1,0:T(8,128)(2,1)S(1)} %get-tuple-element.14.own_pick, f32[256,128]{1,0:T(8,128)S(1)} %filter.1.own, bf16[256,256]{1,0:T(8,128)(2,1)S(1)} %get-tuple-element.15.back), custom_call_target="tpu_custom_call" | custom-call | tf_op jit(solution)/shard_map/margin/pallas_call | solution.py:435
  31.5 33.3 %all_to_all.5 = f32[64,8,128]{2,1,0:T(8,128)S(1)} all-to-all(f32[64,8,128]{2,1,0:T(8,128)S(1)} %bitcast.7), channel_id=1, replica_groups=mesh['dom'=64,'band'=4] {'dom'}, dimensions={0} | all-to-all | bytes 524288 | tf_op jit(solution)/shard_map/all_to_all | solution.py:445
  64.8 0.7 %reduce_sum.9 = f32[8,128]{1,0:T(8,128)} reduce(f32[64,8,128]{2,1,0:T(8,128)S(1)} %all_to_all.5, f32[]{:T(128)} %constant.10.clone.1), dimensions={0}, to_apply=%region_0.0 | reduce | flops 64512 | bytes 266244 | tf_op jit(solution)/shard_map/reduce_sum | solution.py:446
  (3 shorter events, 0.0 us)
Async XLA Ops:
  3.0 7.1 %collective-permute-start.1 = (f32[280,128]{1,0:T(8,128)}, f32[280,128]{1,0:T(8,128)S(1)}, u32[]{:S(2)}, u32[]{:S(2)}) collective-permute-start(f32[280,128]{1,0:T(8,128)} %get-tuple-element.10.packed), channel_id=1, source_target_pairs={{0,12},{12,0},{4,8},{8,4},{16,28},{28,16},{20,24},{24,20},{32,44},... | collective-permute-start | bytes 430088 | tf_op jit(solution)/shard_map/ppermute | solution.py:353
  6.1 7.5 %collective-permute-start.2 = (f32[280,128]{1,0:T(8,128)}, f32[280,128]{1,0:T(8,128)S(1)}, u32[]{:S(2)}, u32[]{:S(2)}) collective-permute-start(f32[280,128]{1,0:T(8,128)} %get-tuple-element.10.packed), channel_id=1, source_target_pairs={{8,20},{20,8},{12,16},{16,12},{24,36},{36,24},{28,32},{32,28},{40,... | collective-permute-start | bytes 430088 | tf_op jit(solution)/shard_map/ppermute | solution.py:353
  6.7 8.6 %collective-permute-start = (f32[280,128]{1,0:T(8,128)}, f32[280,128]{1,0:T(8,128)S(1)}, u32[]{:S(2)}, u32[]{:S(2)}) collective-permute-start(f32[280,128]{1,0:T(8,128)} %get-tuple-element.10.packed), channel_id=1, source_target_pairs={{0,4},{4,0},{8,12},{12,8},{16,20},{20,16},{24,28},{28,24},{32,36},... | collective-permute-start | bytes 430088 | tf_op jit(solution)/shard_map/ppermute | solution.py:353
  7.0 3.5 %copy-start.2 = (f32[8,256]{1,0:T(8,128)S(1)}, f32[8,256]{1,0:T(8,128)}, u32[]{:S(2)}) copy-start(f32[8,256]{1,0:T(8,128)} %get-tuple-element.11.rank) | copy-start | bytes 24580
  10.1 5.6 %collective-permute-start.3 = (f32[280,128]{1,0:T(8,128)S(1)}, f32[280,128]{1,0:T(8,128)S(1)}, u32[]{:S(2)}, u32[]{:S(2)}) collective-permute-start(f32[280,128]{1,0:T(8,128)S(1)} %collective-permute-done.1.got_a), channel_id=1, source_target_pairs={{0,4},{4,0},{8,12},{12,8},{16,20},{20,16},{24,28},{28,24},{32,36},... | collective-permute-start | bytes 430088 | tf_op jit(solution)/shard_map/ppermute | solution.py:353
  10.4 0.7 %copy-start.3 = (s32[512]{0:T(512)S(1)}, s32[512]{0:T(512)}, u32[]{:S(2)}) copy-start(s32[512]{0:T(512)} %param.11) | copy-start | bytes 6148
  11.1 0.9 %copy-start = (f32[280,128]{1,0:T(8,128)S(1)}, f32[280,128]{1,0:T(8,128)}, u32[]{:S(2)}) copy-start(f32[280,128]{1,0:T(8,128)} %get-tuple-element.10.packed) | copy-start | bytes 430084
  13.6 5.2 %copy-start.1 = (f32[280,128]{1,0:T(8,128)S(1)}, f32[280,128]{1,0:T(8,128)}, u32[]{:S(2)}) copy-start(f32[280,128]{1,0:T(8,128)} %get-tuple-element.10.packed) | copy-start | bytes 430084
  13.6 5.2 %collective-permute-start.4 = (f32[280,128]{1,0:T(8,128)S(1)}, f32[280,128]{1,0:T(8,128)S(1)}, u32[]{:S(2)}, u32[]{:S(2)}) collective-permute-start(f32[280,128]{1,0:T(8,128)S(1)} %collective-permute-done.2.got_b), channel_id=1, source_target_pairs={{0,4},{4,0},{8,12},{12,8},{16,20},{20,16},{24,28},{28,24},{32,36},... | collective-permute-start | bytes 430088 | tf_op jit(solution)/shard_map/ppermute | solution.py:353

commit v7 on v4

--- a/solution.py
+++ b/solution.py
@@ -335,8 +335,8 @@
     own_high = dot(high, own_pick[...]).astype(bf16)
     own_low = dot(low, own_pick[...]).astype(bf16)
     part = cross(own_high, high) + cross(own_high, low) + cross(own_low, high)
-    chosen = [dot(term, pick[...]) for term in exact(part)]
-    out[...] = (chosen[0] + chosen[1] + chosen[2]).T
+    chosen = [dot(term, pick[...]) for term in split(part)]
+    out[...] = (chosen[0] + chosen[1]).T
     copy.wait()
 
 

time: 65.8 us -> 65.7 us (level)
  no operation moved by 1% of the time
where the time goes in v7:
time: 65.7 us; the launch traced here: 65.5 us
  blocking collectives  40.6 us (62%)
  Pallas kernels  11.7 us (18%)
  starting transfers between devices  6.09 us (9%)
  waiting for transfers between devices  4.07 us (6%)
  local copies, waits for them, and re-layouts  1.59 us (2%)
  other arithmetic  0.74 us (1%)
  between operations  0.7 us (1%)
    all_to_all x1, blocking collectives, shards(): lax.all_to_all(term.reshape(doms, rows, width), 'dom', 0, 0, tiled=True)  33.3 us
    all_gather x1, blocking collectives, shards(): all_states = lax.all_gather(by_layer, 'band', axis=1, tiled=True)  7.34 us
    ppermute x5, starting transfers between devices, swapped(): return lax.ppermute(block, axis, route)  6.09 us
    ppermute x5, waiting for transfers between devices, swapped(): return lax.ppermute(block, axis, route)  4.07 us
    pallas_call x1, Pallas kernels, shards(): pl.pallas_call(filter_kernel, out_shape=jax.ShapeDtypeStruct((nodes, widt...  4.02 us
    pallas_call x1, Pallas kernels, shards(): pl.pallas_call(sort_kernel, out_shape=[jax.ShapeDtypeStruct((nodes + EXTR...  2.43 us
    pallas_call x1, Pallas kernels, shards(): pl.pallas_call(near_kernel, out_shape=jax.ShapeDtypeStruct((3 * LAYERS, 1...  2.37 us
    unnamed x8, local copies, waits for them, and re-layouts  1.59 us
  transfers between devices with their start and end apart: 5, of which 3 were waited for; matrix products, arithmetic and copies ran while one was open for 0% of the time, Pallas kernels for 6%

profile of v7, /device:TPU:32, one launch (start us, length us, event | category | flops | bytes accessed | tf_op | source)
XLA Modules:
  0.0 65.5 jit_solution(5748020107985843870)
XLA Ops:
  0.6 2.4 %sort.1 = (f32[280,128]{1,0:T(8,128)}, f32[8,256]{1,0:T(8,128)}) custom-call(f32[256,128]{1,0:T(8,128)} %field.1, s32[8,256]{1,0:T(8,128)} %links.1, f32[1,256]{1,0:T(1,128)} %bitcast.9, f32[1,256]{1,0:T(1,128)} %bitcast.10, s32[1,64]{1,0:T(1,128)} %bitcast.11), custom_call_target="tpu_custom_call" | custom-call | tf_op jit(solution)/shard_map/sort/pallas_call | solution.py:362
  3.1 3.1 %collective-permute-start.1 = (f32[280,128]{1,0:T(8,128)}, f32[280,128]{1,0:T(8,128)S(1)}, u32[]{:S(2)}, u32[]{:S(2)}) collective-permute-start(f32[280,128]{1,0:T(8,128)} %get-tuple-element.10.packed), channel_id=1, source_target_pairs={{0,12},{12,0},{4,8},{8,4},{16,28},{28,16},{20,24},{24,20},{32,44},... | collective-permute-start | bytes 430088 | tf_op jit(solution)/shard_map/ppermute | solution.py:348
  6.2 0.7 %collective-permute-start.2 = (f32[280,128]{1,0:T(8,128)}, f32[280,128]{1,0:T(8,128)S(1)}, u32[]{:S(2)}, u32[]{:S(2)}) collective-permute-start(f32[280,128]{1,0:T(8,128)} %get-tuple-element.10.packed), channel_id=1, source_target_pairs={{8,20},{20,8},{12,16},{16,12},{24,36},{36,24},{28,32},{32,28},{40,... | collective-permute-start | bytes 430088 | tf_op jit(solution)/shard_map/ppermute | solution.py:348
  6.8 0.2 collective-permute-start
  7.1 3.1 %collective-permute-done.1.got_a = f32[280,128]{1,0:T(8,128)S(1)} collective-permute-done((f32[280,128]{1,0:T(8,128)}, f32[280,128]{1,0:T(8,128)S(1)}, u32[]{:S(2)}, u32[]{:S(2)}) %collective-permute-start.1) | collective-permute-done | bytes 143392 | tf_op jit(solution)/shard_map/ppermute | solution.py:348
  10.1 0.3 collective-permute-start.3
  10.4 0.1 pad_add_fusion.place
  10.5 0.0 copy-done.2
  10.5 0.7 %copy-done.3 = s32[512]{0:T(512)S(1)} copy-done((s32[512]{0:T(512)S(1)}, s32[512]{0:T(512)}, u32[]{:S(2)}) %copy-start.3) | copy-done | bytes 2072
  11.2 0.9 %copy-done = f32[280,128]{1,0:T(8,128)S(1)} copy-done((f32[280,128]{1,0:T(8,128)S(1)}, f32[280,128]{1,0:T(8,128)}, u32[]{:S(2)}) %copy-start) | copy-done | bytes 143384
  12.1 1.5 %own.1 = (f32[4,128,128]{2,1,0:T(8,128)S(1)}, bf16[256,256]{1,0:T(8,128)(2,1)S(1)}, bf16[512,512]{1,0:T(8,128)(2,1)S(1)}, bf16[512,128]{1,0:T(8,128)(2,1)S(1)}) custom-call(s32[2]{0:T(128)S(1)} %pad_add_fusion.place, f32[280,128]{1,0:T(8,128)S(1)} %copy-done, f32[8,256]{1,0:T(8,128)S(1)} %copy-done.2, s32[1,512]{1,0:T(1,128)S(1)} %bitcast.8), custom_call_target="tpu_custom_call" | custom-call | flops 1000000000 | bytes 1000000 | tf_op jit(solution)/shard_map/own/pallas_call | solution.py:385
  13.6 0.0 copy-start.1
  13.6 0.0 collective-permute-done.2.got_b
  13.6 1.8 %collective-permute-start.4 = (f32[280,128]{1,0:T(8,128)S(1)}, f32[280,128]{1,0:T(8,128)S(1)}, u32[]{:S(2)}, u32[]{:S(2)}) collective-permute-start(f32[280,128]{1,0:T(8,128)S(1)} %collective-permute-done.2.got_b), channel_id=1, source_target_pairs={{0,4},{4,0},{8,12},{12,8},{16,20},{20,16},{24,28},{28,24},{32,36},... | collective-permute-start | bytes 430088 | tf_op jit(solution)/shard_map/ppermute | solution.py:348
  15.5 0.0 collective-permute-done.inner
  15.5 0.3 collective-permute-done.3.relay_a
  15.7 2.4 %near.1.near_cells = f32[12,128,128]{2,1,0:T(8,128)S(1)} custom-call(s32[2]{0:T(128)S(1)} %pad_add_fusion.place, f32[280,128]{1,0:T(8,128)S(1)} %collective-permute-done.inner, f32[280,128]{1,0:T(8,128)S(1)} %collective-permute-done.1.got_a, f32[280,128]{1,0:T(8,128)S(1)} %collective-permute-done.2.got_b, f32[280,128]{1,0:T(8,128)S(1)} %collective-permute-done.3.relay_a), custom_call_target="tpu_custom_call" | custom-call | flops 2000000000 | bytes 1000000 | tf_op jit(solution)/shard_map/near/pallas_call | solution.py:400
  18.1 0.7 %collective-permute-done.4.relay_b = f32[280,128]{1,0:T(8,128)S(1)} collective-permute-done((f32[280,128]{1,0:T(8,128)S(1)}, f32[280,128]{1,0:T(8,128)S(1)}, u32[]{:S(2)}, u32[]{:S(2)}) %collective-permute-start.4) | collective-permute-done | bytes 143392 | tf_op jit(solution)/shard_map/ppermute | solution.py:348
  18.8 4.0 %filter.1.own = f32[256,128]{1,0:T(8,128)S(1)} custom-call(s32[2]{0:T(128)S(1)} %pad_add_fusion.place, f32[280,128]{1,0:T(8,128)S(1)} %copy-done.1, f32[280,128]{1,0:T(8,128)S(1)} %collective-permute-done.inner, f32[280,128]{1,0:T(8,128)S(1)} %collective-permute-done.1.got_a, f32[280,128]{1,0:T(8,128)S(1)} %collective-permute-done.2.got_b, ...), custom_call_target="tpu_custom_call" | custom-call | tf_op jit(solution)/shard_map/filter/pallas_call | solution.py:411
  22.9 7.3 %all_gather.3.states = f32[256,512]{1,0:T(8,128)S(1)} all-gather(f32[256,128]{1,0:T(8,128)S(1)} %filter.1.own), channel_id=1, replica_groups=mesh['dom'=64,'band'=4] {'band'}, dimensions={1}, use_global_device_ids=true | all-gather | bytes 655360 | tf_op jit(solution)/shard_map/all_gather | solution.py:429
  30.2 1.4 %margin.1 = (f32[512,128]{1,0:T(8,128)S(1)}, f32[256,128]{1,0:T(8,128)}) custom-call(f32[256,512]{1,0:T(8,128)S(1)} %all_gather.3.states, bf16[512,512]{1,0:T(8,128)(2,1)S(1)} %get-tuple-element.13.pick, bf16[512,128]{1,0:T(8,128)(2,1)S(1)} %get-tuple-element.14.own_pick, f32[256,128]{1,0:T(8,128)S(1)} %filter.1.own, bf16[256,256]{1,0:T(8,128)(2,1)S(1)} %get-tuple-element.15.back), custom_call_target="tpu_custom_call" | custom-call | tf_op jit(solution)/shard_map/margin/pallas_call | solution.py:430
  31.6 33.3 %all_to_all.5 = f32[64,8,128]{2,1,0:T(8,128)S(1)} all-to-all(f32[64,8,128]{2,1,0:T(8,128)S(1)} %bitcast.7), channel_id=1, replica_groups=mesh['dom'=64,'band'=4] {'dom'}, dimensions={0} | all-to-all | bytes 524288 | tf_op jit(solution)/shard_map/all_to_all | solution.py:440
  64.8 0.1 reduce_sum.9
  64.9 0.6 broadcast_multiply_fusion
  (4 shorter events, 0.0 us)
Async XLA Ops:
  3.1 7.1 %collective-permute-start.1 = (f32[280,128]{1,0:T(8,128)}, f32[280,128]{1,0:T(8,128)S(1)}, u32[]{:S(2)}, u32[]{:S(2)}) collective-permute-start(f32[280,128]{1,0:T(8,128)} %get-tuple-element.10.packed), channel_id=1, source_target_pairs={{0,12},{12,0},{4,8},{8,4},{16,28},{28,16},{20,24},{24,20},{32,44},... | collective-permute-start | bytes 430088 | tf_op jit(solution)/shard_map/ppermute | solution.py:348
  6.2 7.5 %collective-permute-start.2 = (f32[280,128]{1,0:T(8,128)}, f32[280,128]{1,0:T(8,128)S(1)}, u32[]{:S(2)}, u32[]{:S(2)}) collective-permute-start(f32[280,128]{1,0:T(8,128)} %get-tuple-element.10.packed), channel_id=1, source_target_pairs={{8,20},{20,8},{12,16},{16,12},{24,36},{36,24},{28,32},{32,28},{40,... | collective-permute-start | bytes 430088 | tf_op jit(solution)/shard_map/ppermute | solution.py:348
  6.8 8.6 %collective-permute-start = (f32[280,128]{1,0:T(8,128)}, f32[280,128]{1,0:T(8,128)S(1)}, u32[]{:S(2)}, u32[]{:S(2)}) collective-permute-start(f32[280,128]{1,0:T(8,128)} %get-tuple-element.10.packed), channel_id=1, source_target_pairs={{0,4},{4,0},{8,12},{12,8},{16,20},{20,16},{24,28},{28,24},{32,36},... | collective-permute-start | bytes 430088 | tf_op jit(solution)/shard_map/ppermute | solution.py:348
  7.1 3.5 %copy-start.2 = (f32[8,256]{1,0:T(8,128)S(1)}, f32[8,256]{1,0:T(8,128)}, u32[]{:S(2)}) copy-start(f32[8,256]{1,0:T(8,128)} %get-tuple-element.11.rank) | copy-start | bytes 24580
  10.1 5.6 %collective-permute-start.3 = (f32[280,128]{1,0:T(8,128)S(1)}, f32[280,128]{1,0:T(8,128)S(1)}, u32[]{:S(2)}, u32[]{:S(2)}) collective-permute-start(f32[280,128]{1,0:T(8,128)S(1)} %collective-permute-done.1.got_a), channel_id=1, source_target_pairs={{0,4},{4,0},{8,12},{12,8},{16,20},{20,16},{24,28},{28,24},{32,36},... | collective-permute-start | bytes 430088 | tf_op jit(solution)/shard_map/ppermute | solution.py:348
  10.5 0.7 %copy-start.3 = (s32[512]{0:T(512)S(1)}, s32[512]{0:T(512)}, u32[]{:S(2)}) copy-start(s32[512]{0:T(512)} %param.11) | copy-start | bytes 6148
  11.2 0.9 %copy-start = (f32[280,128]{1,0:T(8,128)S(1)}, f32[280,128]{1,0:T(8,128)}, u32[]{:S(2)}) copy-start(f32[280,128]{1,0:T(8,128)} %get-tuple-element.10.packed) | copy-start | bytes 430084
  13.6 5.2 %copy-start.1 = (f32[280,128]{1,0:T(8,128)S(1)}, f32[280,128]{1,0:T(8,128)}, u32[]{:S(2)}) copy-start(f32[280,128]{1,0:T(8,128)} %get-tuple-element.10.packed) | copy-start | bytes 430084
  13.6 5.2 %collective-permute-start.4 = (f32[280,128]{1,0:T(8,128)S(1)}, f32[280,128]{1,0:T(8,128)S(1)}, u32[]{:S(2)}, u32[]{:S(2)}) collective-permute-start(f32[280,128]{1,0:T(8,128)S(1)} %collective-permute-done.2.got_b), channel_id=1, source_target_pairs={{0,4},{4,0},{8,12},{12,8},{16,20},{20,16},{24,28},{28,24},{32,36},... | collective-permute-start | bytes 430088 | tf_op jit(solution)/shard_map/ppermute | solution.py:348
